TPU v7x, 256 devices: a whole 4x4x8 slice. The times are simulated.
256 devices in a mesh: row: 16 (over x, y_lo, core), col: 16 (over y_hi, z).
Axes of the slice: x: 4, y: 4 (y_hi: 2, y_lo: 2; y = y_hi * 2 + y_lo), z: 8, core: 2. Of those that a mesh axis runs over, the one named last changes fastest.
Arguments:
- tcc_before: bfloat16 [16384, 16384], P('row', 'col'), as said below
- shift_panel: bfloat16 [16384, 512], P(('row', 'col')), may hold values from -0.046875 to 0.046875
- source_map: float32 [1024], replicated, may hold values from 0.1 to 1
- pixels: int32 [512], replicated, may hold values from 0 to 1023
- start_vectors: float32 [16384, 128], P(('row', 'col')), may hold values from -6 to 6
Outputs:
- filtered: float32 [16384, 128], P(('row', 'col'))
- tcc: bfloat16 [16384, 16384], P('row', 'col')
Inputs may be any that keep to these rules, and one draw needn't show every extreme that they name: tcc_before is exactly symmetric.
All inputs are finite; a program needn't handle non-finite values.
Results may differ from a plain program's by a relative error of at most 0.022.
Values may be sent and summed in bfloat16 or wider, within the bound.
A program may use at most 64 MiB of HBM per device.

v0:
```python
import jax
import jax.numpy as jnp
from jax import lax
from jax.sharding import PartitionSpec as P

DEGREES = 4


CENTER = 0.45
HALF_WIDTH = 1.6


def partner(shard, axis, stride):
    return lax.ppermute(shard, axis, [(i, i ^ 1 << stride) for i in range(lax.axis_size(axis))])


def from_root(block, axis, owner):
    block = jnp.where(lax.axis_index(axis) == owner, block, jnp.zeros_like(block))
    return lax.psum(block, axis)


def on_device(tcc_before, shift_panel, source_map, pixels, start_vectors):
    n_row = lax.axis_size("row")
    n_col = lax.axis_size("col")
    ratio = n_row // n_col
    row_index = lax.axis_index("row")
    col_index = lax.axis_index("col")
    hit = pixels[:, None] == jnp.arange(source_map.shape[0], dtype=jnp.int32)[None, :]
    weight = jnp.sum(jnp.where(hit, source_map[None, :], jnp.float32(0.0)), axis=1)
    scaled = (shift_panel.astype(jnp.float32) * jnp.sqrt(weight)[None, :]).astype(jnp.bfloat16)
    own_rows = lax.all_gather(scaled, "col", axis=0, tiled=True)
    opposite = partner(own_rows, "row", n_row.bit_length() - 2)
    turned_own = jnp.where(row_index < n_row // 2, -opposite, opposite)
    left = jnp.concatenate([own_rows, turned_own], axis=1)
    pieces = from_root(left, "row", col_index * ratio + 0)
    update = lax.dot_general(
        left, pieces, (((1,), (1,)), ((), ())), preferred_element_type=jnp.float32
    )
    tile = (tcc_before.astype(jnp.float32) + update).astype(jnp.bfloat16)

    def apply_fixed(current_b):
        row_block = lax.all_gather(current_b, "col", axis=0, tiled=True)
        parts = from_root(row_block, "row", col_index * ratio + 0)
        image = lax.psum_scatter(
            jnp.dot(tile, parts, preferred_element_type=jnp.float32).astype(jnp.bfloat16),
            "col",
            scatter_dimension=0,
            tiled=True,
        ).astype(jnp.float32)
        return image - CENTER * current_b.astype(jnp.float32)

    previous = start_vectors
    current_b = previous.astype(jnp.bfloat16)
    current = apply_fixed(current_b) / HALF_WIDTH
    for degree in range(1, DEGREES):
        current_b = current.astype(jnp.bfloat16)
        following = 2.0 / HALF_WIDTH * apply_fixed(current_b) - previous
        previous, current = (current, following)
    return (current, tile)


def solution(mesh):
    in_specs = (P("row", "col"), P(("row", "col"), None), P(), P(), P(("row", "col"), None))
    out_specs = (P(("row", "col"), None), P("row", "col"))
    return jax.shard_map(
        on_device, mesh=mesh, in_specs=in_specs, out_specs=out_specs, check_vma=False
    )
```

profile of v0, /device:TPU:1, one launch (start us, length us, event | category | flops | bytes accessed | tf_op | source)
XLA Modules:
  0.0 1546.6 jit_solution(8580080202011614042)
XLA Ops:
  7.2 1.0 select_reduce_fusion
  8.3 1.5 multiply_convert_fusion
  9.8 80.2 %all-gather.2.cloned.1.call-done = bf16[1024,512]{1,0:T(8,128)(2,1)} async-done(((bf16[64,512]{1,0:T(8,128)(2,1)}), bf16[1024,512]{1,0:T(8,128)(2,1)}) %all-gather.2.cloned.1.call-update) | async-done | bytes 1048592 | tf_op jit(solution)/shard_map/all_gather | solution.py:31
  90.1 2.7 collective-permute-start
  93.5 31.4 %all_gather.16 = bf16[1024,128]{1,0:T(8,128)(2,1)S(1)} all-gather(bf16[64,128]{1,0:T(8,128)(2,1)S(1)} %convert_element_type.64), channel_id=1, replica_groups=mesh['row'=16,'col'=16] {'col'}, dimensions={0}, use_global_device_ids=true | all-gather | bytes 278528 | tf_op jit(solution)/shard_map/all_gather | solution.py:42
  125.8 1.8 broadcast_select_fusion
  127.6 135.2 %all-reduce.12.cloned.1.call-done = (bf16[1024,1024]{1,0:T(8,128)(2,1)}, bf16[1024,128]{1,0:T(8,128)(2,1)}) async-done(((bf16[1024,1024]{1,0:T(8,128)(2,1)}, bf16[1024,128]{1,0:T(8,128)(2,1)}), (bf16[1024,1024]{1,0:T(8,128)(2,1)}, bf16[1024,128]{1,0:T(8,128)(2,1)})) %all-reduce.12.cloned.1.call-update) | async-done | bytes 2359312 | tf_op jit(solution)/shard_map/psum | solution.py:19
  262.8 4.9 add_convert_fusion
  267.8 1.5 convolution_convert_fusion.3
  269.3 192.3 %reduce-scatter.5.cloned.1.call-done = bf16[64,128]{1,0:T(8,128)(2,1)} async-done(((bf16[1024,128]{1,0:T(8,128)(2,1)}), bf16[64,128]{1,0:T(8,128)(2,1)}) %reduce-scatter.5.cloned.1.call-update) | async-done | bytes 16400 | tf_op jit(solution)/shard_map/reduce_scatter | solution.py:44
  462.4 32.4 %all_gather.17 = bf16[1024,128]{1,0:T(8,128)(2,1)S(1)} all-gather(bf16[64,128]{1,0:T(8,128)(2,1)S(1)} %fusion), channel_id=1, replica_groups=mesh['row'=16,'col'=16] {'col'}, dimensions={0}, use_global_device_ids=true | all-gather | bytes 278528 | tf_op jit(solution)/shard_map/all_gather | solution.py:42
  495.6 129.4 %all-reduce.6.cloned.1.call-done = bf16[1024,128]{1,0:T(8,128)(2,1)} async-done(((bf16[1024,128]{1,0:T(8,128)(2,1)}), bf16[1024,128]{1,0:T(8,128)(2,1)}) %all-reduce.6.cloned.1.call-update) | async-done | bytes 262160 | tf_op jit(solution)/shard_map/psum | solution.py:19
  625.0 2.4 convolution_convert_fusion.2
  627.4 193.2 %reduce-scatter.7.cloned.1.call-done = bf16[64,128]{1,0:T(8,128)(2,1)} async-done(((bf16[1024,128]{1,0:T(8,128)(2,1)}), bf16[64,128]{1,0:T(8,128)(2,1)}) %reduce-scatter.7.cloned.1.call-update) | async-done | bytes 16400 | tf_op jit(solution)/shard_map/reduce_scatter | solution.py:44
  821.5 32.4 %all_gather.18 = bf16[1024,128]{1,0:T(8,128)(2,1)S(1)} all-gather(bf16[64,128]{1,0:T(8,128)(2,1)S(1)} %fusion.1), channel_id=1, replica_groups=mesh['row'=16,'col'=16] {'col'}, dimensions={0}, use_global_device_ids=true | all-gather | bytes 278528 | tf_op jit(solution)/shard_map/all_gather | solution.py:42
  854.6 129.3 %all-reduce.8.cloned.1.call-done = bf16[1024,128]{1,0:T(8,128)(2,1)} async-done(((bf16[1024,128]{1,0:T(8,128)(2,1)}), bf16[1024,128]{1,0:T(8,128)(2,1)}) %all-reduce.8.cloned.1.call-update) | async-done | bytes 262160 | tf_op jit(solution)/shard_map/psum | solution.py:19
  983.9 2.4 convolution_convert_fusion.1
  986.4 193.3 %reduce-scatter.9.cloned.1.call-done = bf16[64,128]{1,0:T(8,128)(2,1)} async-done(((bf16[1024,128]{1,0:T(8,128)(2,1)}), bf16[64,128]{1,0:T(8,128)(2,1)}) %reduce-scatter.9.cloned.1.call-update) | async-done | bytes 16400 | tf_op jit(solution)/shard_map/reduce_scatter | solution.py:44
  1179.7 0.8 subtract_convert_fusion
  1180.5 32.4 %all_gather.19 = bf16[1024,128]{1,0:T(8,128)(2,1)S(1)} all-gather(bf16[64,128]{1,0:T(8,128)(2,1)S(1)} %subtract_convert_fusion), channel_id=1, replica_groups=mesh['row'=16,'col'=16] {'col'}, dimensions={0}, use_global_device_ids=true | all-gather | bytes 278528 | tf_op jit(solution)/shard_map/all_gather | solution.py:42
  1213.7 129.2 %all-reduce.10.cloned.1.call-done = bf16[1024,128]{1,0:T(8,128)(2,1)} async-done(((bf16[1024,128]{1,0:T(8,128)(2,1)}), bf16[1024,128]{1,0:T(8,128)(2,1)}) %all-reduce.10.cloned.1.call-update) | async-done | bytes 262160 | tf_op jit(solution)/shard_map/psum | solution.py:19
  1343.0 2.4 convolution_convert_fusion
  1345.3 193.4 %reduce-scatter.11.cloned.1.call-done = bf16[64,128]{1,0:T(8,128)(2,1)} async-done(((bf16[1024,128]{1,0:T(8,128)(2,1)}), bf16[64,128]{1,0:T(8,128)(2,1)}) %reduce-scatter.11.cloned.1.call-update) | async-done | bytes 16400 | tf_op jit(solution)/shard_map/reduce_scatter | solution.py:44
  1538.7 1.4 multiply_subtract_fusion
  (42 shorter events, 5.9 us)
Async XLA Ops:
  7.2 82.9 %all-gather.2.cloned.1.call-start = ((), (), s32[]{:S(2)}) async-start(), calls=%async_computation.4 | async-start | bytes 1114112 | tf_op jit(solution)/shard_map/all_gather | solution.py:31
  9.8 253.0 %all-reduce.12.cloned.1.call-start = ((), (), s32[]{:S(2)}) async-start(), calls=%async_computation.12 | async-start | bytes 4718592 | tf_op jit(solution)/shard_map/psum | solution.py:19
  90.1 35.7 %copy-start.1 = (bf16[1024,512]{1,0:T(8,128)(2,1)S(1)}, bf16[1024,512]{1,0:T(8,128)(2,1)}, u32[]{:S(2)}) copy-start(bf16[1024,512]{1,0:T(8,128)(2,1)} %all-gather.2.cloned.1.call-done) | copy-start | bytes 3145732
  90.1 35.6 %collective-permute-start = (bf16[1024,512]{1,0:T(8,128)(2,1)}, bf16[1024,512]{1,0:T(8,128)(2,1)S(1)}, u32[]{:S(2)}, u32[]{:S(2)}) collective-permute-start(bf16[1024,512]{1,0:T(8,128)(2,1)} %all-gather.2.cloned.1.call-done), channel_id=1, source_target_pairs={{0,128},{16,144},{32,160},{48,176},{64,192},{80,208},{96,224},{112... | collective-permute-start | bytes 3145736 | tf_op jit(solution)/shard_map/ppermute | solution.py:14
  127.6 334.0 %reduce-scatter.5.cloned.1.call-start = ((), (), s32[]{:S(2)}) async-start(), calls=%async_computation.5 | async-start | bytes 278528 | tf_op jit(solution)/shard_map/reduce_scatter | solution.py:44
  262.8 5.0 copy-start.3
  267.7 1075.2 %copy-start = (bf16[1024,1024]{1,0:T(8,128)(2,1)}, bf16[1024,1024]{1,0:T(8,128)(2,1)S(1)}, u32[]{:S(2)}) copy-start(bf16[1024,1024]{1,0:T(8,128)(2,1)S(1)} %add_convert_fusion) | copy-start | bytes 6291460
  267.8 193.9 %copy-start.2 = (f32[64,128]{1,0:T(8,128)S(1)}, f32[64,128]{1,0:T(8,128)}, u32[]{:S(2)}) copy-start(f32[64,128]{1,0:T(8,128)} %param.9) | copy-start | bytes 98308
  269.3 355.7 %all-reduce.6.cloned.1.call-start = ((), (), s32[]{:S(2)}) async-start(), calls=%async_computation.6 | async-start | bytes 524288 | tf_op jit(solution)/shard_map/psum | solution.py:19
  461.6 359.0 %copy-start.4 = (bf16[64,128]{1,0:T(8,128)(2,1)S(1)}, bf16[64,128]{1,0:T(8,128)(2,1)}, u32[]{:S(2)}) copy-start(bf16[64,128]{1,0:T(8,128)(2,1)} %reduce-scatter.5.cloned.1.call-done) | copy-start | bytes 49156
  495.6 325.1 %reduce-scatter.7.cloned.1.call-start = ((), (), s32[]{:S(2)}) async-start(), calls=%async_computation.7 | async-start | bytes 278528 | tf_op jit(solution)/shard_map/reduce_scatter | solution.py:44
  627.4 356.6 %all-reduce.8.cloned.1.call-start = ((), (), s32[]{:S(2)}) async-start(), calls=%async_computation.8 | async-start | bytes 524288 | tf_op jit(solution)/shard_map/psum | solution.py:19
  820.6 359.1 %copy-start.5 = (bf16[64,128]{1,0:T(8,128)(2,1)S(1)}, bf16[64,128]{1,0:T(8,128)(2,1)}, u32[]{:S(2)}) copy-start(bf16[64,128]{1,0:T(8,128)(2,1)} %reduce-scatter.7.cloned.1.call-done) | copy-start | bytes 49156
  854.6 325.1 %reduce-scatter.9.cloned.1.call-start = ((), (), s32[]{:S(2)}) async-start(), calls=%async_computation.9 | async-start | bytes 278528 | tf_op jit(solution)/shard_map/reduce_scatter | solution.py:44
  986.3 356.7 %all-reduce.10.cloned.1.call-start = ((), (), s32[]{:S(2)}) async-start(), calls=%async_computation.10 | async-start | bytes 524288 | tf_op jit(solution)/shard_map/psum | solution.py:19
  1179.7 359.0 %copy-start.6 = (bf16[64,128]{1,0:T(8,128)(2,1)S(1)}, bf16[64,128]{1,0:T(8,128)(2,1)}, u32[]{:S(2)}) copy-start(bf16[64,128]{1,0:T(8,128)(2,1)} %reduce-scatter.9.cloned.1.call-done) | copy-start | bytes 49156
  1213.7 325.1 %reduce-scatter.11.cloned.1.call-start = ((), (), s32[]{:S(2)}) async-start(), calls=%async_computation.11 | async-start | bytes 278528 | tf_op jit(solution)/shard_map/reduce_scatter | solution.py:44
Sparse Core Ops, SparseCore 0:
  11.2 78.8 all-gather.1
  127.7 135.0 all-reduce.11
  269.4 192.2 reduce-scatter.4
  495.7 129.2 all-reduce.5
  628.6 191.9 reduce-scatter.6
  854.7 129.1 all-reduce.7
  987.7 191.9 reduce-scatter.8
  1213.8 129.1 all-reduce.9
  1346.8 191.9 reduce-scatter.10
where the time goes:
time: 1550 us
  waiting for transfers between devices  1380 us (89%)
  blocking collectives  129 us (8%)
    reduce_scatter x4, waiting for transfers between devices, apply_fixed(): lax.psum_scatter(jnp.dot(tile, parts, preferred_element_type=jnp.float32)...  772 us
    psum x4, waiting for transfers between devices, from_root(): return lax.psum(block, axis)  523 us
    all_gather x4, blocking collectives, apply_fixed(): row_block = lax.all_gather(current_b, 'col', axis=0, tiled=True)  129 us
    all_gather x1, waiting for transfers between devices, on_device(): own_rows = lax.all_gather(scaled, 'col', axis=0, tiled=True)  80.2 us
  transfers between devices with their start and end apart: 10, of which 9 were waited for; matrix products, arithmetic and copies ran while one was open for 0% of the time, Pallas kernels for 0%

commit v1 on v0

v1 whole, which is shorter than its diff:
```python
import jax
import jax.numpy as jnp
from jax import lax
from jax.experimental import pallas as pl
from jax.experimental.pallas import tpu as pltpu
from jax.sharding import PartitionSpec as P

DEGREES = 4
CENTER = 0.45
HALF_WIDTH = 1.6
MESH = pl.DeviceIdType.MESH
N = 16
ROWS = 64
f32 = jnp.float32
bf16 = jnp.bfloat16


def mod(value, size):
    return lax.rem(value + size, size)


def device(x, y, core, z):
    x, y, z = mod(x, 4), mod(y, 4), mod(z, 8)
    return (4 * x + 2 * lax.rem(y, 2) + core, 8 * (y // 2) + z)


def body(
    before, panel, source, pixels, start, filtered, tcc,
    left, right, tile, gathered, partial, arrived, outgoing,
    tcc_sem, quad_send, quad_recv, ring_send, ring_recv, turn_send, turn_recv,
    block_send, block_recv, gather_send, gather_recv, sum_send, sum_recv,
):
    row, col = lax.axis_index("row"), lax.axis_index("col")
    x, y_lo, core = row // 4, lax.rem(row // 2, 2), lax.rem(row, 2)
    y_hi, z = col // 8, lax.rem(col, 8)
    y = 2 * y_hi + y_lo
    half = x // 2
    kind = lax.rem(row, 8)
    a, b, k = z // 4, lax.rem(z // 2, 2), lax.rem(z, 2)

    load = pltpu.make_async_copy(before, tile, tcc_sem.at[0])
    load.start()

    def peer(axis, index):
        return (index, col) if axis == "row" else (row, index)

    barrier = pltpu.get_barrier_semaphore()

    @pl.loop(1, N)
    def _(step):
        pl.semaphore_signal(barrier, 1, device_id=peer("row", mod(row + step, N)), device_id_type=MESH)
        pl.semaphore_signal(barrier, 1, device_id=peer("col", mod(col + step, N)), device_id_type=MESH)

    far = jnp.where(y_lo == 0, y - 1, y + 1)
    pl.semaphore_signal(barrier, 1, device_id=device(x, far + 4, core, z), device_id_type=MESH)
    pl.semaphore_signal(barrier, 1, device_id=device(x + 2, y + 2, core, z), device_id_type=MESH)

    src = jnp.broadcast_to(source[...], (N, source.shape[1]))
    high = src.astype(bf16).astype(f32)
    middle = (src - high).astype(bf16).astype(f32)
    low = src - high - middle
    part = lax.broadcasted_iota(jnp.int32, src.shape, 0)
    parts = jnp.where(part == 0, high, jnp.where(part == 1, middle, jnp.where(part == 2, low, 0.0)))
    place = lax.broadcasted_iota(jnp.int32, (source.shape[1], pixels.shape[1]), 0)
    hit = jnp.where(place == pixels[...], 1.0, 0.0).astype(bf16)
    three = jnp.dot(parts.astype(bf16), hit, preferred_element_type=f32)
    weight = three[0:1] + three[1:2] + three[2:3]
    scaled = (panel[...].astype(f32) * jnp.sqrt(weight)).astype(bf16)
    left[half, y_hi, z] = scaled
    outgoing[0] = start[...].astype(bf16)

    @pl.when(kind == z)
    def _():
        right[half, y_hi, z] = scaled

    pl.semaphore_wait(barrier, 2 * (N - 1) + 2)

    def remote(src_ref, dst_ref, send, recv, to):
        return pltpu.make_async_remote_copy(
            src_ref=src_ref, dst_ref=dst_ref, send_sem=send, recv_sem=recv, device_id=to, device_id_type=MESH
        )

    own = left.at[half, y_hi, z]

    def quad_place(q):
        return mod(half + q % 2, 2), mod(y_hi + q // 2, 2)

    def quad(q):
        return remote(own, own, quad_send.at[q], quad_recv.at[q], device(x + 2 * (q % 2), y + 2 * (q // 2), core, z))

    def quad_wait(q):
        there = left.at[quad_place(q)[0], quad_place(q)[1], z]
        remote(there, there, quad_send.at[q], quad_recv.at[q], (row, col)).wait_recv()

    for q in (1, 2, 3):
        quad(q).start()

    def turn():
        return remote(own, right.at[half, y_hi, z], turn_send.at[0], turn_recv.at[z], device(x, y, core, kind))

    @pl.when(kind != z)
    def _():
        turn().start()

    def ring(way, step, q):
        h, yh = quad_place(q)
        at = left.at[h, yh, mod(z - step if way == 0 else z + step, 8) if step else z]
        return remote(
            at, at, ring_send.at[way, step, q], ring_recv.at[way, step, q],
            device(x, y, core, z + 1 if way == 0 else z + 7),
        )

    def ring_wait(way, step, q):
        h, yh = quad_place(q)
        at = left.at[h, yh, mod(z - step - 1 if way == 0 else z + step + 1, 8)]
        remote(at, at, ring_send.at[way, step, q], ring_recv.at[way, step, q], (row, col)).wait_recv()

    def ring_step(step):
        for q in range(4):
            if step == 0 and q > 0:
                quad_wait(q)
            for way in (0, 1):
                if step > 0:
                    ring_wait(way, step - 1, q)
                if step < 3 or (q < 2) == (way == 0):
                    ring(way, step, q).start()

    x_match, y_match, holder = lax.rem(x, 2) == a, y_lo == b, core == k
    near = jnp.where(x_match, half, mod(x + 3, 4) // 2)
    down, up = mod(y + 3, 4) // 2, mod(y + 1, 4) // 2

    def turns(i):
        mine = (near if i < 2 else 1 - near, i % 2)
        other = ((near, 1 - near, near, 1 - near)[i], (0, 1, 1, 0)[i])
        return jnp.where(x_match, mine[0], other[0]), jnp.where(x_match, mine[1], other[1])

    def block(h, yh, p):
        return right.at[h, yh, pl.ds(4 * p, 4)]

    def block_copy(h, yh, p, way):
        to = (
            device(x + 1, y, core, z), device(x + 3, y, core, z),
            device(x, y + 1, core, z), device(x, y + 3, core, z), device(x, y, 1 - core, z),
        )[way]
        at = block(h, yh, p)
        index = 4 * h + 2 * yh + p
        return remote(at, at, block_send.at[index, way], block_recv.at[index], to)

    def block_wait(h, yh, p):
        at = block(h, yh, p)
        remote(at, at, block_send.at[0, 0], block_recv.at[4 * h + 2 * yh + p], (row, col)).wait_recv()

    def flow(op):
        starting = op == "start"

        def go(*which):
            copy = block_copy(*which)
            copy.start() if starting else copy.wait_send()

        def arrive(*which):
            if starting:
                block_wait(*which)

        def first():
            @pl.when(x_match & y_match & holder)
            def _():
                if starting:
                    @pl.loop(1, 8)
                    def _(step):
                        other = mod(z + step, 8)
                        at = right.at[half, y_hi, other]
                        remote(at, at, turn_send.at[0], turn_recv.at[other], (row, col)).wait_recv()
                for p, way in ((0, 0), (1, 1), (1, 0), (0, 1)):
                    go(half, y_hi, p, way)
                for p in (0, 1):
                    for way in (2, 3, 4):
                        go(half, y_hi, p, way)

        def second():
            @pl.when(jnp.logical_not(x_match) & y_match & holder)
            def _():
                for i in range(2):
                    h, p = turns(i)
                    arrive(h, y_hi, p)
                    go(h, y_hi, p, i)
                    for way in (2, 3, 4):
                        go(h, y_hi, p, way)

        def third():
            @pl.when(y_match & holder)
            def _():
                for i in range(2, 4):
                    h, p = turns(i)
                    arrive(h, y_hi, p)
                    for way in (2, 3, 4):
                        go(h, y_hi, p, way)

        def fourth():
            @pl.when(jnp.logical_not(y_match) & holder)
            def _():
                for i in range(4):
                    h, p = turns(i)
                    for yh, way in ((down, 2), (up, 3)):
                        arrive(h, yh, p)
                        passing = h == (0 if way == 2 else 1)

                        @pl.when(passing)
                        def _():
                            go(h, yh, p, way)

                        go(h, yh, p, 4)

        def fifth():
            @pl.when(y_match & holder)
            def _():
                for i in range(4):
                    h, p = turns(i)
                    arrive(h, 1 - y_hi, p)
                    go(h, 1 - y_hi, p, 4)

        return first, second, third, fourth, fifth

    first, second, third, fourth, fifth = flow("start")
    ring_step(0)
    first()
    ring_step(1)
    second()
    ring_step(2)
    third()
    ring_step(3)

    def gather_start(stage, axis):
        me = row if axis == "row" else col
        piece = pl.ds(pl.multiple_of(me * ROWS, ROWS), ROWS)
        gathered[stage, piece] = outgoing[stage]

        @pl.loop(1, N)
        def _(step):
            to = mod(me + step, N)
            remote(
                outgoing.at[stage], gathered.at[stage, piece], gather_send.at[stage, to], gather_recv.at[stage, me],
                peer(axis, to),
            ).start()

    def gather_wait(stage, axis):
        me = row if axis == "row" else col

        @pl.loop(1, N)
        def _(step):
            other = mod(me + step, N)
            at = gathered.at[stage, pl.ds(pl.multiple_of(other * ROWS, ROWS), ROWS)]
            remote(at, at, gather_send.at[stage, other], gather_recv.at[stage, other], (row, col)).wait_recv()

    def sum_send_piece(stage, axis, to):
        me = row if axis == "row" else col
        return remote(
            partial.at[stage, pl.ds(pl.multiple_of(to * ROWS, ROWS), ROWS)], arrived.at[stage, me],
            sum_send.at[stage, to], sum_recv.at[stage, me], peer(axis, to),
        )

    def sum_wait(stage, axis, total):
        me = row if axis == "row" else col

        def add(step, total):
            other = mod(me + step, N)
            at = arrived.at[stage, other]
            remote(at, at, sum_send.at[stage, other], sum_recv.at[stage, other], (row, col)).wait_recv()
            return total + at[...].astype(f32)

        return lax.fori_loop(1, N, add, total)

    gather_start(0, "col")
    fourth()
    fifth()
    for q in range(4):
        for way in (0, 1):
            if (q < 2) == (way == 0):
                ring_wait(way, 3, q)

    @pl.when(jnp.logical_not(holder))
    def _():
        for h in range(2):
            for yh in range(2):
                for p in range(2):
                    block_wait(h, yh, p)

    load.wait()
    sign = jnp.where(half == y_hi, 1.0, -1.0).astype(f32)
    nt = (((1,), (1,)), ((), ()))

    @pl.loop(0, 8)
    def _(i):
        yh, zs = i // 4, pl.ds(2 * lax.rem(i, 4), 2)
        span = pl.ds(pl.multiple_of(i * 128, 128), 128)
        straight = lax.dot_general(
            left[half, yh, zs].reshape(128, 512), right[y_hi].reshape(1024, 512), nt, preferred_element_type=f32
        )
        turned = lax.dot_general(
            left[1 - half, yh, zs].reshape(128, 512), right[1 - y_hi].reshape(1024, 512), nt,
            preferred_element_type=f32,
        )
        tile[span] = (tile[span].astype(f32) + (straight + sign * turned)).astype(bf16)

    store = pltpu.make_async_copy(tile, tcc, tcc_sem.at[1])
    store.start()

    centre = jnp.where(row == col, CENTER, 0.0).astype(f32)
    mine = []
    for stage in range(DEGREES):
        axis, over = ("col", "row") if stage % 2 == 0 else ("row", "col")
        me = row if over == "row" else col
        if stage > 0:
            gather_start(stage, axis)
        gather_wait(stage, axis)
        vectors = gathered.at[stage]
        if stage % 2 == 0:
            turned_vectors = vectors[...].T
        for i in range(4):
            span = pl.ds(256 * i, 256)
            if stage % 2 == 0:
                image = jnp.dot(turned_vectors, tile[:, span], preferred_element_type=f32).T
            else:
                image = jnp.dot(tile[span], vectors[...], preferred_element_type=f32)
            image = image - centre * vectors[span].astype(f32)
            partial[stage, span] = image.astype(bf16)
            for j in range(4):
                to = 4 * i + j

                @pl.when(me == to)
                def _():
                    filtered[...] = image[ROWS * j:ROWS * (j + 1)]

                @pl.when(me != to)
                def _():
                    sum_send_piece(stage, over, to).start()
        total = sum_wait(stage, over, filtered[...])
        if stage == 0:
            current = total / HALF_WIDTH
        else:
            current = 2.0 / HALF_WIDTH * total - (mine[stage - 2] if stage > 1 else start[...])
        mine.append(current)
        if stage < DEGREES - 1:
            outgoing[stage + 1] = current.astype(bf16)
    filtered[...] = mine[-1]

    store.wait()
    for q in (1, 2, 3):
        quad(q).wait_send()

    @pl.when(kind != z)
    def _():
        turn().wait_send()

    for step in range(4):
        for q in range(4):
            for way in (0, 1):
                if step < 3 or (q < 2) == (way == 0):
                    ring(way, step, q).wait_send()
    for part_of in flow("wait"):
        part_of()
    for stage in range(DEGREES):
        axis, over = ("col", "row") if stage % 2 == 0 else ("row", "col")

        @pl.loop(1, N)
        def _(step):
            to = mod((row if axis == "row" else col) + step, N)
            at = outgoing.at[stage]
            remote(at, at, gather_send.at[stage, to], gather_recv.at[stage, to], (row, col)).wait_send()
            to = mod((row if over == "row" else col) + step, N)
            sum_send_piece(stage, over, to).wait_send()


def on_device(tcc_before, shift_panel, source_map, pixels, start_vectors):
    vmem = pl.BlockSpec(memory_space=pltpu.VMEM)
    anywhere = pl.BlockSpec(memory_space=pl.ANY)
    dma = pltpu.SemaphoreType.DMA
    return pl.pallas_call(
        body,
        out_shape=(
            jax.ShapeDtypeStruct(start_vectors.shape, f32),
            jax.ShapeDtypeStruct(tcc_before.shape, bf16),
        ),
        in_specs=[anywhere, vmem, vmem, vmem, vmem],
        out_specs=(vmem, anywhere),
        scratch_shapes=[
            pltpu.VMEM((2, 2, 8, ROWS, 512), bf16),
            pltpu.VMEM((2, 2, 8, ROWS, 512), bf16),
            pltpu.VMEM((1024, 1024), bf16),
            pltpu.VMEM((DEGREES, 1024, 128), bf16),
            pltpu.VMEM((DEGREES, 1024, 128), bf16),
            pltpu.VMEM((DEGREES, N, ROWS, 128), bf16),
            pltpu.VMEM((DEGREES, ROWS, 128), bf16),
            dma((2,)), dma((4,)), dma((4,)), dma((2, 4, 4)), dma((2, 4, 4)), dma((1,)), dma((8,)),
            dma((8, 5)), dma((8,)), dma((DEGREES, N)), dma((DEGREES, N)), dma((DEGREES, N)), dma((DEGREES, N)),
        ],
        compiler_params=pltpu.CompilerParams(
            collective_id=0, has_side_effects=True, vmem_limit_bytes=40 * 1024 * 1024
        ),
    )(tcc_before, shift_panel, source_map.reshape(1, -1), pixels.reshape(1, -1), start_vectors)


def solution(mesh):
    in_specs = (P("row", "col"), P(("row", "col"), None), P(), P(), P(("row", "col"), None))
    out_specs = (P(("row", "col"), None), P("row", "col"))
    return jax.shard_map(
        on_device, mesh=mesh, in_specs=in_specs, out_specs=out_specs, check_vma=False
    )
```

time: 1550 us -> 116 us (0.07)
  the two profiles are of different devices: /device:TPU:1 before, /device:TPU:24 now
where the time goes in v1:
time: 116 us
  Pallas kernels  109 us (94%)
  local copies, waits for them, and re-layouts  6.48 us (6%)
    pallas_call x1, Pallas kernels, on_device(): pl.pallas_call(body, out_shape=(jax.ShapeDtypeStruct(start_vectors.shape,...  109 us
    unnamed x12, local copies, waits for them, and re-layouts  6.48 us

profile of v1, /device:TPU:24, one launch (start us, length us, event | category | flops | bytes accessed | tf_op | source)
XLA Modules:
  0.0 116.2 jit_solution(474953253180686032)
XLA Ops:
  0.6 0.0 copy-start
  0.6 1.6 %copy-done = bf16[1024,1024]{1,0:T(8,128)(2,1)S(1)} copy-done((bf16[1024,1024]{1,0:T(8,128)(2,1)S(1)}, bf16[1024,1024]{1,0:T(8,128)(2,1)}, u32[]{:S(2)}) %copy-start) | copy-done | bytes 2097176
  2.2 0.0 copy-start.1
  2.2 0.8 copy-done.1
  3.1 0.0 copy-start.2
  3.1 0.8 copy-done.2
  3.8 0.0 copy-start.3
  3.8 0.7 copy-done.3
  4.5 0.0 copy-start.4
  4.5 0.7 copy-done.4
  5.2 109.0 %shard_map.68 = (f32[64,128]{1,0:T(8,128)S(1)}, bf16[1024,1024]{1,0:T(8,128)(2,1)S(1)}) custom-call(bf16[1024,1024]{1,0:T(8,128)(2,1)S(1)} %copy-done, bf16[64,512]{1,0:T(8,128)(2,1)S(1)} %copy-done.1, f32[1,1024]{1,0:T(1,128)S(1)} %bitcast.2, s32[1,512]{1,0:T(1,128)S(1)} %bitcast.3, f32[64,128]{1,0:T(8,128)S(1)} %copy-done.2), custom_call_target="tpu_custom_call" | custom-call | tf_op jit(solution)/shard_map/pallas_call | solution.py:377
  114.2 0.6 copy.9
  114.8 1.3 %copy.10 = bf16[1024,1024]{1,0:T(8,128)(2,1)} copy(bf16[1024,1024]{1,0:T(8,128)(2,1)S(1)} %get-tuple-element.5) | data formatting | bytes 4194304
Async XLA Ops:
  0.6 1.6 %copy-start = (bf16[1024,1024]{1,0:T(8,128)(2,1)S(1)}, bf16[1024,1024]{1,0:T(8,128)(2,1)}, u32[]{:S(2)}) copy-start(bf16[1024,1024]{1,0:T(8,128)(2,1)} %before.1) | copy-start | bytes 6291460
  2.2 0.8 copy-start.1
  3.1 0.8 copy-start.2
  3.8 0.7 copy-start.3
  4.5 0.7 copy-start.4

commit v2 on v0

v2 whole, which is shorter than its diff:
```python
import jax
import jax.numpy as jnp
from jax import lax
from jax.experimental import pallas as pl
from jax.experimental.pallas import tpu as pltpu
from jax.sharding import PartitionSpec as P

DEGREES = 4
CENTER = 0.45
HALF_WIDTH = 1.6
MESH = pl.DeviceIdType.MESH
N = 16
ROWS = 64
ZONE = 512
WINDOW = 2


def farthest_first(moves, hops):
    return sorted(moves, key=lambda move: -hops(*move))


ALONG_Z = (4, 3, -3, 2, -2, 1, -1, 0)
COL_MOVES = farthest_first(
    [(dy, dz) for dy in (1, 0) for dz in ALONG_Z if dy or dz], lambda dy, dz: 2 * dy + abs(dz)
)
ROW_MOVES = farthest_first(
    [(dx, dy, dk) for dx in (2, 1, -1, 0) for dy in (1, 0) for dk in (1, 0) if dx or dy or dk],
    lambda dx, dy, dk: abs(dx) + dy,
)
PLANE_MOVES = [move for move in ROW_MOVES if move[2] == 0]
f32 = jnp.float32
bf16 = jnp.bfloat16


def mod(value, size):
    return lax.rem(value + size, size)


def device(x, y, core, z):
    x, y, z = mod(x, 4), mod(y, 4), mod(z, 8)
    return (4 * x + 2 * lax.rem(y, 2) + core, 8 * (y // 2) + z)


def body(
    before, panel_in, source_in, pixels_in, start_in, filtered_out, tcc,
    panel, source, pixels, start, filtered, left, right, tile, gathered, partial, arrived, outgoing,
    whole, history,
    tcc_sem, quad_send, quad_recv, ring_send, ring_recv, turn_send,
    piece_send, piece_recv, gather_send, gather_recv, pass_send, pass_recv, sum_send, sum_recv,
):
    row, col = lax.axis_index("row"), lax.axis_index("col")
    x, y_lo, core = row // 4, lax.rem(row // 2, 2), lax.rem(row, 2)
    y_hi, z = col // 8, lax.rem(col, 8)
    y = 2 * y_hi + y_lo
    half = x // 2
    kind = lax.rem(row, 8)
    here = (row, col)
    sibling = (row + 1 - 2 * core, col)

    loads = [
        pltpu.make_async_copy(src, dst, tcc_sem.at[2 + i])
        for i, (src, dst) in enumerate(
            ((pixels_in, pixels), (source_in, source), (panel_in, panel), (start_in, start))
        )
    ]
    for small in loads:
        small.start()
    load = pltpu.make_async_copy(before, tile, tcc_sem.at[0])
    load.start()

    barrier = pltpu.get_barrier_semaphore()

    @pl.loop(1, N)
    def _(step):
        pl.semaphore_signal(barrier, 1, device_id=(mod(row + step, N), col), device_id_type=MESH)
        pl.semaphore_signal(barrier, 1, device_id=(row, mod(col + step, N)), device_id_type=MESH)

    far = jnp.where(y_lo == 0, y - 1, y + 1)
    swapped = (8 * half + z, 8 * y_hi + kind)
    for to in (device(x, far + 4, core, z), device(x + 2, y + 2, core, z), swapped):
        pl.semaphore_signal(barrier, 1, device_id=to, device_id_type=MESH)

    for small in loads:
        small.wait()
    src = jnp.broadcast_to(source[...], (N, source.shape[1]))
    high = src.astype(bf16).astype(f32)
    middle = (src - high).astype(bf16).astype(f32)
    low = src - high - middle
    part = lax.broadcasted_iota(jnp.int32, src.shape, 0)
    parts = jnp.where(part == 0, high, jnp.where(part == 1, middle, jnp.where(part == 2, low, 0.0)))
    place = lax.broadcasted_iota(jnp.int32, (source.shape[1], pixels.shape[1]), 0)
    hit = jnp.where(place == pixels[...], 1.0, 0.0).astype(bf16)
    three = jnp.dot(parts.astype(bf16), hit, preferred_element_type=f32)
    weight = three[0:1] + three[1:2] + three[2:3]
    scaled = (panel[...].astype(f32) * jnp.sqrt(weight)).astype(bf16)
    left[half, y_hi, z, :, :ZONE] = scaled
    left[half, y_hi, z, :, ZONE:] = start[...].astype(bf16)

    @pl.when(kind == z)
    def _():
        right[half, y_hi, z] = scaled

    pl.semaphore_wait(barrier, 2 * (N - 1) + 3)

    def remote(src_ref, dst_ref, send, recv, to):
        return pltpu.make_async_remote_copy(
            src_ref=src_ref, dst_ref=dst_ref, send_sem=send, recv_sem=recv, device_id=to, device_id_type=MESH
        )

    def turn():
        return remote(
            left.at[half, y_hi, z, :, pl.ds(0, ZONE)], right.at[half, y_hi, z], turn_send.at[0],
            piece_recv.at[half, y_hi, z], swapped,
        )

    @pl.when(kind != z)
    def _():
        turn().start()

    def chip(i, j):
        along_x, along_y = jnp.where(core == 0, i, j), jnp.where(core == 0, j, i)
        return mod(x + along_x, 4), mod(y + along_y, 4)

    def place_of(cx, cy, k):
        return cx // 2, cy // 2, 4 * lax.rem(cx, 2) + 2 * lax.rem(cy, 2) + k

    def piece_copy(i, j, way):
        at = place_of(*chip(i, j), core)
        if way is None:
            index, to = 6, sibling
        else:
            tx, ty = chip(*way)
            index, to = (way[0] or 3 + way[1]) - 1, device(tx, ty, core, z)
        return remote(right.at[at], right.at[at], piece_send.at[i, j, index], piece_recv.at[at], to)

    def piece_wait(i, j, k=None):
        cx, cy = chip(i, j)
        at = place_of(cx, cy, core if k is None else k)
        remote(right.at[at], right.at[at], turn_send.at[0], piece_recv.at[at], here).wait_recv()

    def piece_first():
        @pl.when(kind != z)
        def _():
            piece_wait(0, 0)

        for d in (2, 1, 3):
            piece_copy(0, 0, (d, 0)).start()
        for d in (2, 1, 3):
            piece_copy(0, 0, (0, d)).start()
        piece_copy(0, 0, None).start()

    def piece_second():
        for i in (1, 3, 2):
            piece_wait(i, 0)
            for d in (2, 1, 3):
                piece_copy(i, 0, (0, d)).start()
            piece_copy(i, 0, None).start()

    def piece_third():
        for i in (0, 1, 3, 2):
            for j in (1, 3, 2):
                piece_wait(i, j)
                piece_copy(i, j, None).start()

    def piece_last():
        for i in range(4):
            for j in range(4):
                piece_wait(i, j, 1 - core)

    def piece_sent():
        for i in range(4):
            for j in range(4):
                piece_copy(i, j, None).wait_send()
                if j == 0:
                    for d in (1, 2, 3):
                        piece_copy(i, 0, (0, d)).wait_send()
                        if i == 0:
                            piece_copy(0, 0, (d, 0)).wait_send()

    def piece_of(q, zz):
        h, yh = mod(half + q % 2, 2), mod(y_hi + q // 2, 2)
        return left.at[h, yh, zz] if q % 2 == 0 else left.at[h, yh, zz, :, pl.ds(0, ZONE)]

    def quad(q):
        own = left.at[half, y_hi, z]
        own = own if q % 2 == 0 else left.at[half, y_hi, z, :, pl.ds(0, ZONE)]
        return remote(own, own, quad_send.at[q], quad_recv.at[q], device(x + 2 * (q % 2), y + 2 * (q // 2), core, z))

    def quad_wait(q):
        there = piece_of(q, z)
        remote(there, there, quad_send.at[q], quad_recv.at[q], here).wait_recv()

    def ring(way, step, q):
        at = piece_of(q, mod(z - step if way == 0 else z + step, 8))
        return remote(
            at, at, ring_send.at[way, step, q], ring_recv.at[way, step, q],
            device(x, y, core, z + 1 if way == 0 else z + 7),
        )

    def ring_wait(way, step, q):
        at = piece_of(q, mod(z - step - 1 if way == 0 else z + step + 1, 8))
        remote(at, at, ring_send.at[way, step, q], ring_recv.at[way, step, q], here).wait_recv()

    in_flight = [[], []]

    def ring_start(way, step, q):
        if len(in_flight[way]) == WINDOW:
            ring(way, *in_flight[way].pop(0)).wait_send()
        ring(way, step, q).start()
        in_flight[way].append((step, q))

    def ring_step(step):
        for q in range(4):
            if step == 0 and q > 0:
                quad_wait(q)
            for way in (0, 1):
                if step > 0:
                    ring_wait(way, step - 1, q)
                if step < 3 or (q < 2) == (way == 0):
                    ring_start(way, step, q)

    for q in (1, 2, 3):
        quad(q).start()
    ring_step(0)
    piece_first()
    ring_step(1)
    piece_second()
    ring_step(2)
    piece_third()
    ring_step(3)
    piece_last()
    load.wait()
    for q in range(4):
        for way in (0, 1):
            if (q < 2) == (way == 0):
                ring_wait(way, 3, q)

    sign = jnp.where(half == y_hi, 1.0, -1.0).astype(f32)
    nt = (((1,), (1,)), ((), ()))

    @pl.loop(0, 4)
    def _(i):
        yh, zs = i // 2, pl.ds(4 * lax.rem(i, 2), 4)
        span = pl.ds(pl.multiple_of(i * 256, 256), 256)
        straight = lax.dot_general(
            left[half, yh, zs, :, :ZONE].reshape(256, ZONE), right[y_hi].reshape(1024, ZONE), nt,
            preferred_element_type=f32,
        )
        turned = lax.dot_general(
            left[1 - half, yh, zs, :, :ZONE].reshape(256, ZONE), right[1 - y_hi].reshape(1024, ZONE), nt,
            preferred_element_type=f32,
        )
        tile[span] = (tile[span].astype(f32) + (straight + sign * turned)).astype(bf16)

    store = pltpu.make_async_copy(tile, tcc, tcc_sem.at[1])
    store.start()

    def member(axis, move):
        if axis == "row":
            dx, dy, dk = move
            return 4 * mod(x + dx, 4) + 2 * mod(y_lo + dy, 2) + mod(core + dk, 2)
        dy, dz = move
        return 8 * mod(y_hi + dy, 2) + mod(z + dz, 8)

    def back(axis, move):
        return tuple(-d for d in move)

    def address(axis, index):
        return (index, col) if axis == "row" else (row, index)

    def rows_of(index):
        return pl.ds(pl.multiple_of(index * ROWS, ROWS), ROWS)

    most = pl.ds(0, (N - 1) * ROWS)

    def gather_col(stage):
        def copy(move):
            at = gathered.at[stage, rows_of(col)]
            return remote(
                outgoing.at[stage], at, gather_send.at[stage], gather_recv.at[stage], address("col", member("col", move))
            )

        gathered[stage, rows_of(col)] = outgoing[stage]
        for move in COL_MOVES:
            copy(move).start()

        def wait():
            every = gathered.at[stage, most]
            remote(every, every, gather_send.at[stage], gather_recv.at[stage], here).wait()

        return wait

    def gather_row(stage):
        which = stage // 2

        def copy(n, move):
            at = gathered.at[stage, rows_of(row)]
            return remote(
                outgoing.at[stage], at, pass_send.at[which, n], pass_recv.at[which, n],
                address("row", member("row", move)),
            )

        def across(n, move):
            at = gathered.at[stage, rows_of(member("row", back("row", move)))]
            return remote(at, at, pass_send.at[which, 7 + n], pass_recv.at[which, 7 + n], sibling)

        gathered[stage, rows_of(row)] = outgoing[stage]
        across(7, (0, 0, 0)).start()
        for n, move in enumerate(PLANE_MOVES):
            copy(n, move).start()

        def wait():
            for n, move in reversed(list(enumerate(PLANE_MOVES))):
                at = gathered.at[stage, rows_of(member("row", back("row", move)))]
                remote(at, at, pass_send.at[which, n], pass_recv.at[which, n], here).wait_recv()
                across(n, move).start()
            for n in range(8):
                move = PLANE_MOVES[n] if n < 7 else (0, 0, 0)
                at = gathered.at[stage, rows_of(row + 1 - 2 * core)]
                remote(at, at, pass_send.at[which, n], pass_recv.at[which, 7 + n], here).wait_recv()
            for n, move in enumerate(PLANE_MOVES):
                copy(n, move).wait_send()
                across(n, move).wait_send()
            across(7, (0, 0, 0)).wait_send()

        return wait

    def sum_start(stage, axis):
        for n, move in enumerate(ROW_MOVES if axis == "row" else COL_MOVES):
            to = member(axis, move)
            remote(
                partial.at[stage, rows_of(to)], arrived.at[stage, n], sum_send.at[stage], sum_recv.at[stage],
                address(axis, to),
            ).start()

    def sum_wait(stage):
        every = arrived.at[stage]
        remote(every, every, sum_send.at[stage], sum_recv.at[stage], here).wait()

    centre = jnp.where(row == col, CENTER, 0.0).astype(f32)
    for stage in range(DEGREES):
        over = "row" if stage % 2 == 0 else "col"
        me = row if over == "row" else col
        if stage == 0:
            vectors = left[half, :, :, :, ZONE:].reshape(1024, 128)
        else:
            wait = gather_col(stage) if stage % 2 == 0 else gather_row(stage)
            wait()
            vectors = gathered[stage]
        if stage % 2 == 0:
            image = jnp.dot(vectors.T, tile[...], preferred_element_type=f32).T
        else:
            image = jnp.dot(tile[...], vectors, preferred_element_type=f32)
        image = image - centre * vectors.astype(f32)
        partial[stage] = image.astype(bf16)
        whole[...] = image
        sum_start(stage, over)
        own = whole[rows_of(me)]
        sum_wait(stage)
        total = own + jnp.sum(arrived[stage].astype(f32), axis=0)
        if stage == 0:
            following = total / HALF_WIDTH
        else:
            following = 2.0 / HALF_WIDTH * total - (start[...] if stage == 1 else history[stage - 2])
        if stage < DEGREES - 1:
            outgoing[stage + 1] = following.astype(bf16)
            history[stage] = following
        else:
            filtered[...] = following

    last = pltpu.make_async_copy(filtered, filtered_out, tcc_sem.at[6])
    last.start()

    for q in (1, 2, 3):
        quad(q).wait_send()

    @pl.when(kind != z)
    def _():
        turn().wait_send()

    for way in (0, 1):
        for step, q in in_flight[way]:
            ring(way, step, q).wait_send()
    piece_sent()
    store.wait()
    last.wait()


def on_device(tcc_before, shift_panel, source_map, pixels, start_vectors):
    anywhere = pl.BlockSpec(memory_space=pl.ANY)
    dma = pltpu.SemaphoreType.DMA
    return pl.pallas_call(
        body,
        out_shape=(
            jax.ShapeDtypeStruct(start_vectors.shape, f32),
            jax.ShapeDtypeStruct(tcc_before.shape, bf16),
        ),
        in_specs=[anywhere] * 5,
        out_specs=(anywhere, anywhere),
        scratch_shapes=[
            pltpu.VMEM((ROWS, 512), bf16),
            pltpu.VMEM((1, 1024), f32),
            pltpu.VMEM((1, 512), jnp.int32),
            pltpu.VMEM((ROWS, 128), f32),
            pltpu.VMEM((ROWS, 128), f32),
            pltpu.VMEM((2, 2, 8, ROWS, ZONE + 128), bf16),
            pltpu.VMEM((2, 2, 8, ROWS, ZONE), bf16),
            pltpu.VMEM((1024, 1024), bf16),
            pltpu.VMEM((DEGREES, 1024, 128), bf16),
            pltpu.VMEM((DEGREES, 1024, 128), bf16),
            pltpu.VMEM((DEGREES, N - 1, ROWS, 128), bf16),
            pltpu.VMEM((DEGREES, ROWS, 128), bf16),
            pltpu.VMEM((1024, 128), f32),
            pltpu.VMEM((DEGREES - 1, ROWS, 128), f32),
            dma((7,)), dma((4,)), dma((4,)), dma((2, 4, 4)), dma((2, 4, 4)), dma((1,)),
            dma((4, 4, 7)), dma((2, 2, 8)), dma((DEGREES,)), dma((DEGREES,)), dma((2, 15)), dma((2, 15)),
            dma((DEGREES,)), dma((DEGREES,)),
        ],
        compiler_params=pltpu.CompilerParams(
            collective_id=0, has_side_effects=True, vmem_limit_bytes=60 * 1024 * 1024
        ),
    )(tcc_before, shift_panel, source_map.reshape(1, -1), pixels.reshape(1, -1), start_vectors)


def solution(mesh):
    in_specs = (P("row", "col"), P(("row", "col"), None), P(), P(), P(("row", "col"), None))
    out_specs = (P(("row", "col"), None), P("row", "col"))
    return jax.shard_map(
        on_device, mesh=mesh, in_specs=in_specs, out_specs=out_specs, check_vma=False
    )
```

time: 1550 us -> 101 us (0.07)
  waiting for transfers between devices: 1380 us -> 0 us
  blocking collectives: 129 us -> 0 us
  Pallas kernels: 0 us -> 95.8 us
    reduce_scatter x4 -> x0, waiting for transfers between devices: 772 us -> none  [apply_fixed(): lax.psum_scatter(jnp.dot(tile, parts, preferred_element_type=jnp.float32)...]
    psum x4 -> x0, waiting for transfers between devices: 523 us -> none  [from_root(): return lax.psum(block, axis)]
    all_gather x4 -> x0, blocking collectives: 129 us -> none  [apply_fixed(): row_block = lax.all_gather(current_b, 'col', axis=0, tiled=True)]
    pallas_call x0 -> x1, Pallas kernels: none -> 95.8 us  [on_device(): pl.pallas_call(body, out_shape=(jax.ShapeDtypeStruct(start_vectors.shape,...]
    all_gather x1 -> x0, waiting for transfers between devices: 80.2 us -> none  [on_device(): own_rows = lax.all_gather(scaled, 'col', axis=0, tiled=True)]
  transfers between devices with their start and end apart: 10 -> 0, of which waited for: 9 -> 0; matrix products, arithmetic and copies ran while one was open for 0% -> 0% of each run, Pallas kernels for 0% -> 0%
where the time goes in v2:
time: 101 us
  Pallas kernels  95.8 us (95%)
  local copies, waits for them, and re-layouts  4.45 us (4%)
    pallas_call x1, Pallas kernels, on_device(): pl.pallas_call(body, out_shape=(jax.ShapeDtypeStruct(start_vectors.shape,...  95.8 us
    unnamed x2, local copies, waits for them, and re-layouts  4.45 us

profile of v2, /device:TPU:1, one launch (start us, length us, event | category | flops | bytes accessed | tf_op | source)
XLA Modules:
  0.0 100.9 jit_solution(5148973673428528689)
XLA Ops:
  0.6 95.8 %shard_map.68 = (f32[64,128]{1,0:T(8,128)}, bf16[1024,1024]{1,0:T(8,128)(2,1)}) custom-call(bf16[1024,1024]{1,0:T(8,128)(2,1)} %before.1, bf16[64,512]{1,0:T(8,128)(2,1)} %panel_in.1, f32[1,1024]{1,0:T(1,128)} %bitcast.2, s32[1,512]{1,0:T(1,128)} %bitcast.3, f32[64,128]{1,0:T(8,128)} %start_in.1), custom_call_target="tpu_custom_call" | custom-call | tf_op jit(solution)/shard_map/pallas_call | solution.py:392
  96.4 1.4 %copy.9 = f32[64,128]{1,0:T(8,128)} copy(f32[64,128]{1,0:T(8,128)} %get-tuple-element.4) | data formatting | bytes 65536
  97.8 3.1 %copy.10 = bf16[1024,1024]{1,0:T(8,128)(2,1)} copy(bf16[1024,1024]{1,0:T(8,128)(2,1)} %get-tuple-element.5) | data formatting | bytes 4194304

commit v3 on v2

--- a/solution.py
+++ b/solution.py
@@ -19,14 +19,12 @@
     return sorted(moves, key=lambda move: -hops(*move))
 
 
-ALONG_Z = (4, 3, -3, 2, -2, 1, -1, 0)
-COL_MOVES = farthest_first(
-    [(dy, dz) for dy in (1, 0) for dz in ALONG_Z if dy or dz], lambda dy, dz: 2 * dy + abs(dz)
-)
 ROW_MOVES = farthest_first(
     [(dx, dy, dk) for dx in (2, 1, -1, 0) for dy in (1, 0) for dk in (1, 0) if dx or dy or dk],
     lambda dx, dy, dk: abs(dx) + dy,
 )
+NEAR = (2, -2, 1, -1)
+OTHERS = ((1, 3), (1, -3), (0, 4), (0, 3), (0, -3), (1, 0))
 PLANE_MOVES = [move for move in ROW_MOVES if move[2] == 0]
 f32 = jnp.float32
 bf16 = jnp.bfloat16
@@ -42,11 +40,11 @@
 
 
 def body(
-    before, panel_in, source_in, pixels_in, start_in, filtered_out, tcc,
-    panel, source, pixels, start, filtered, left, right, tile, gathered, partial, arrived, outgoing,
-    whole, history,
+    before, panel_in, source_in, pixels_in, start_in, filtered, tile,
+    panel, source, pixels, start, left, right, gathered, partial, arrived, outgoing,
+    whole, history, crossed, joined,
     tcc_sem, quad_send, quad_recv, ring_send, ring_recv, turn_send,
-    piece_send, piece_recv, gather_send, gather_recv, pass_send, pass_recv, sum_send, sum_recv,
+    piece_send, piece_recv, gather_send, gather_recv, pass_send, pass_recv, sum_send, sum_recv, cross_recv,
 ):
     row, col = lax.axis_index("row"), lax.axis_index("col")
     x, y_lo, core = row // 4, lax.rem(row // 2, 2), lax.rem(row, 2)
@@ -58,7 +56,7 @@
     sibling = (row + 1 - 2 * core, col)
 
     loads = [
-        pltpu.make_async_copy(src, dst, tcc_sem.at[2 + i])
+        pltpu.make_async_copy(src, dst, tcc_sem.at[1 + i])
         for i, (src, dst) in enumerate(
             ((pixels_in, pixels), (source_in, source), (panel_in, panel), (start_in, start))
         )
@@ -230,30 +228,35 @@
     ring_step(3)
     piece_last()
     load.wait()
+
+    sign = jnp.where(half == y_hi, 1.0, -1.0).astype(f32)
+    nt = (((1,), (1,)), ((), ()))
+
+    def update(yh, quarter):
+        zs = pl.ds(4 * quarter, 4)
+        span = pl.ds(pl.multiple_of(512 * yh + 256 * quarter, 256), 256)
+        straight = lax.dot_general(
+            left[half, yh, zs, :, :ZONE].reshape(256, ZONE), right[y_hi].reshape(1024, ZONE), nt,
+            preferred_element_type=f32,
+        )
+        turned = lax.dot_general(
+            left[1 - half, yh, zs, :, :ZONE].reshape(256, ZONE), right[1 - y_hi].reshape(1024, ZONE), nt,
+            preferred_element_type=f32,
+        )
+        tile[span] = (tile[span].astype(f32) + (straight + sign * turned)).astype(bf16)
+
+    @pl.loop(0, 2)
+    def _(yh):
+        update(yh, z // 4)
+
     for q in range(4):
         for way in (0, 1):
             if (q < 2) == (way == 0):
                 ring_wait(way, 3, q)
 
-    sign = jnp.where(half == y_hi, 1.0, -1.0).astype(f32)
-    nt = (((1,), (1,)), ((), ()))
-
-    @pl.loop(0, 4)
-    def _(i):
-        yh, zs = i // 2, pl.ds(4 * lax.rem(i, 2), 4)
-        span = pl.ds(pl.multiple_of(i * 256, 256), 256)
-        straight = lax.dot_general(
-            left[half, yh, zs, :, :ZONE].reshape(256, ZONE), right[y_hi].reshape(1024, ZONE), nt,
-            preferred_element_type=f32,
-        )
-        turned = lax.dot_general(
-            left[1 - half, yh, zs, :, :ZONE].reshape(256, ZONE), right[1 - y_hi].reshape(1024, ZONE), nt,
-            preferred_element_type=f32,
-        )
-        tile[span] = (tile[span].astype(f32) + (straight + sign * turned)).astype(bf16)
-
-    store = pltpu.make_async_copy(tile, tcc, tcc_sem.at[1])
-    store.start()
+    @pl.loop(0, 2)
+    def _(yh):
+        update(yh, 1 - z // 4)
 
     def member(axis, move):
         if axis == "row":
@@ -271,22 +274,33 @@
     def rows_of(index):
         return pl.ds(pl.multiple_of(index * ROWS, ROWS), ROWS)
 
-    most = pl.ds(0, (N - 1) * ROWS)
+    def piece_ref(stage, index):
+        return partial.at[stage, index // 2, lax.rem(index, 2)]
+
+    partner = (row, member("col", (1, 0)))
 
     def gather_col(stage):
-        def copy(move):
-            at = gathered.at[stage, rows_of(col)]
-            return remote(
-                outgoing.at[stage], at, gather_send.at[stage], gather_recv.at[stage], address("col", member("col", move))
-            )
-
+        at = gathered.at[stage, rows_of(col)]
         gathered[stage, rows_of(col)] = outgoing[stage]
-        for move in COL_MOVES:
-            copy(move).start()
+
+        def copy(recv, move):
+            remote(outgoing.at[stage], at, gather_send.at[0], recv, address("col", member("col", move))).start()
+
+        copy(gather_recv.at[4], (1, 4))
+        for n, dz in enumerate(NEAR):
+            copy(gather_recv.at[n], (0, dz))
+        for move in OTHERS:
+            copy(gather_recv.at[4], move)
 
         def wait():
-            every = gathered.at[stage, most]
-            remote(every, every, gather_send.at[stage], gather_recv.at[stage], here).wait()
+            for n, dz in reversed(list(enumerate(NEAR))):
+                near = gathered.at[stage, rows_of(member("col", (0, -dz)))]
+                remote(near, near, gather_send.at[0], gather_recv.at[n], here).wait_recv()
+                remote(near, near, gather_send.at[0], gather_recv.at[4], partner).start()
+            rest = gathered.at[stage, pl.ds(0, 11 * ROWS)]
+            remote(rest, rest, gather_send.at[0], gather_recv.at[4], here).wait_recv()
+            sent = gathered.at[stage, pl.ds(0, 15 * ROWS)]
+            remote(sent, sent, gather_send.at[0], gather_recv.at[4], here).wait_send()
 
         return wait
 
@@ -325,22 +339,75 @@
 
         return wait
 
-    def sum_start(stage, axis):
-        for n, move in enumerate(ROW_MOVES if axis == "row" else COL_MOVES):
-            to = member(axis, move)
+    def all_sent(stage):
+        every = arrived.at[stage]
+        remote(every, every, sum_send.at[stage], sum_recv.at[stage], here).wait_send()
+
+    def sum_row(stage):
+        which = stage // 2
+        theirs = partial.at[stage, :, 1 - core]
+        remote(theirs, crossed.at[which], sum_send.at[stage], cross_recv.at[which], sibling).start()
+        remote(theirs, crossed.at[which], sum_send.at[stage], cross_recv.at[which], here).wait_recv()
+        both = whole[:, core] + crossed[which].astype(f32)
+        joined[which] = both.astype(bf16)
+        whole[:, core] = both
+        for n, move in enumerate(PLANE_MOVES):
+            to = member("row", move)
             remote(
-                partial.at[stage, rows_of(to)], arrived.at[stage, n], sum_send.at[stage], sum_recv.at[stage],
-                address(axis, to),
+                joined.at[which, to // 2], arrived.at[stage, n], sum_send.at[stage], sum_recv.at[stage],
+                address("row", to),
             ).start()
-
-    def sum_wait(stage):
-        every = arrived.at[stage]
-        remote(every, every, sum_send.at[stage], sum_recv.at[stage], here).wait()
+        if stage == 0:
+            panels_sent()
+        mine = whole[row // 2, core]
+        every = arrived.at[stage, pl.ds(0, 7)]
+        remote(every, every, sum_send.at[stage], sum_recv.at[stage], here).wait_recv()
+        all_sent(stage)
+        return mine + jnp.sum(arrived[stage, :7].astype(f32), axis=0)
+
+    def sum_col(stage):
+        which = 2 + stage // 2
+
+        def copy(src, slot, move):
+            remote(
+                src, arrived.at[stage, slot], sum_send.at[stage], sum_recv.at[stage], address("col", member("col", move))
+            ).start()
+
+        copy(piece_ref(stage, member("col", (1, 4))), 0, (1, 4))
+        for n, dz in enumerate(NEAR):
+            remote(
+                piece_ref(stage, member("col", (1, dz))), crossed.at[which, n], sum_send.at[stage],
+                cross_recv.at[which], partner,
+            ).start()
+        for n, move in enumerate(OTHERS):
+            copy(piece_ref(stage, member("col", move)), 1 + n, move)
+        some = crossed.at[which, pl.ds(0, 4)]
+        remote(some, some, sum_send.at[stage], cross_recv.at[which], here).wait_recv()
+        for n, dz in enumerate(NEAR):
+            to = member("col", (0, dz))
+            joined[which, n] = (whole[to // 2, lax.rem(to, 2)] + crossed[which, n].astype(f32)).astype(bf16)
+            copy(joined.at[which, n], 7 + n, (0, dz))
+        mine = whole[col // 2, lax.rem(col, 2)]
+        every = arrived.at[stage, pl.ds(0, 11)]
+        remote(every, every, sum_send.at[stage], sum_recv.at[stage], here).wait_recv()
+        all_sent(stage)
+        return mine + jnp.sum(arrived[stage, :11].astype(f32), axis=0)
+
+    def panels_sent():
+        for q in (1, 2, 3):
+            quad(q).wait_send()
+
+        @pl.when(kind != z)
+        def _():
+            turn().wait_send()
+
+        for way in (0, 1):
+            for step, q in in_flight[way]:
+                ring(way, step, q).wait_send()
+        piece_sent()
 
     centre = jnp.where(row == col, CENTER, 0.0).astype(f32)
     for stage in range(DEGREES):
-        over = "row" if stage % 2 == 0 else "col"
-        me = row if over == "row" else col
         if stage == 0:
             vectors = left[half, :, :, :, ZONE:].reshape(1024, 128)
         else:
@@ -352,12 +419,9 @@
         else:
             image = jnp.dot(tile[...], vectors, preferred_element_type=f32)
         image = image - centre * vectors.astype(f32)
-        partial[stage] = image.astype(bf16)
-        whole[...] = image
-        sum_start(stage, over)
-        own = whole[rows_of(me)]
-        sum_wait(stage)
-        total = own + jnp.sum(arrived[stage].astype(f32), axis=0)
+        partial[stage] = image.astype(bf16).reshape(8, 2, ROWS, 128)
+        whole[...] = image.reshape(8, 2, ROWS, 128)
+        total = sum_row(stage) if stage % 2 == 0 else sum_col(stage)
         if stage == 0:
             following = total / HALF_WIDTH
         else:
@@ -368,58 +432,44 @@
         else:
             filtered[...] = following
 
-    last = pltpu.make_async_copy(filtered, filtered_out, tcc_sem.at[6])
-    last.start()
-
-    for q in (1, 2, 3):
-        quad(q).wait_send()
-
-    @pl.when(kind != z)
-    def _():
-        turn().wait_send()
-
-    for way in (0, 1):
-        for step, q in in_flight[way]:
-            ring(way, step, q).wait_send()
-    piece_sent()
-    store.wait()
-    last.wait()
-
 
 def on_device(tcc_before, shift_panel, source_map, pixels, start_vectors):
-    anywhere = pl.BlockSpec(memory_space=pl.ANY)
+    hbm = pl.BlockSpec(memory_space=pltpu.HBM)
+    vmem = pl.BlockSpec(memory_space=pltpu.VMEM)
     dma = pltpu.SemaphoreType.DMA
+    operands = (tcc_before, shift_panel, source_map.reshape(1, -1), pixels.reshape(1, -1), start_vectors)
+    operands = [pltpu.with_memory_space_constraint(operand, pltpu.HBM) for operand in operands]
     return pl.pallas_call(
         body,
         out_shape=(
             jax.ShapeDtypeStruct(start_vectors.shape, f32),
             jax.ShapeDtypeStruct(tcc_before.shape, bf16),
         ),
-        in_specs=[anywhere] * 5,
-        out_specs=(anywhere, anywhere),
+        in_specs=[hbm] * 5,
+        out_specs=(vmem, vmem),
         scratch_shapes=[
             pltpu.VMEM((ROWS, 512), bf16),
             pltpu.VMEM((1, 1024), f32),
             pltpu.VMEM((1, 512), jnp.int32),
             pltpu.VMEM((ROWS, 128), f32),
-            pltpu.VMEM((ROWS, 128), f32),
             pltpu.VMEM((2, 2, 8, ROWS, ZONE + 128), bf16),
             pltpu.VMEM((2, 2, 8, ROWS, ZONE), bf16),
-            pltpu.VMEM((1024, 1024), bf16),
             pltpu.VMEM((DEGREES, 1024, 128), bf16),
-            pltpu.VMEM((DEGREES, 1024, 128), bf16),
+            pltpu.VMEM((DEGREES, 8, 2, ROWS, 128), bf16),
             pltpu.VMEM((DEGREES, N - 1, ROWS, 128), bf16),
             pltpu.VMEM((DEGREES, ROWS, 128), bf16),
-            pltpu.VMEM((1024, 128), f32),
+            pltpu.VMEM((8, 2, ROWS, 128), f32),
             pltpu.VMEM((DEGREES - 1, ROWS, 128), f32),
-            dma((7,)), dma((4,)), dma((4,)), dma((2, 4, 4)), dma((2, 4, 4)), dma((1,)),
-            dma((4, 4, 7)), dma((2, 2, 8)), dma((DEGREES,)), dma((DEGREES,)), dma((2, 15)), dma((2, 15)),
-            dma((DEGREES,)), dma((DEGREES,)),
+            pltpu.VMEM((DEGREES, 8, ROWS, 128), bf16),
+            pltpu.VMEM((DEGREES, 8, ROWS, 128), bf16),
+            dma((5,)), dma((4,)), dma((4,)), dma((2, 4, 4)), dma((2, 4, 4)), dma((1,)),
+            dma((4, 4, 7)), dma((2, 2, 8)), dma((1,)), dma((5,)), dma((2, 15)), dma((2, 15)),
+            dma((DEGREES,)), dma((DEGREES,)), dma((DEGREES,)),
         ],
         compiler_params=pltpu.CompilerParams(
-            collective_id=0, has_side_effects=True, vmem_limit_bytes=60 * 1024 * 1024
+            collective_id=0, has_side_effects=True, vmem_limit_bytes=32 * 1024 * 1024
         ),
-    )(tcc_before, shift_panel, source_map.reshape(1, -1), pixels.reshape(1, -1), start_vectors)
+    )(*operands)
 
 
 def solution(mesh):

time: 101 us -> 97.2 us (0.962)
  local copies, waits for them, and re-layouts: 4.45 us -> 1.94 us
  Pallas kernels: 95.8 us -> 94.5 us
    unnamed x2, local copies, waits for them, and re-layouts: 4.45 us -> 1.94 us
    pallas_call x1, Pallas kernels: 95.8 us -> 94.5 us  [on_device(): pl.pallas_call(body, out_shape=(jax.ShapeDtypeStruct(start_vectors.shape,...]
where the time goes in v3:
time: 97.2 us; the launch traced here: 97.1 us
  Pallas kernels  94.5 us (97%)
  local copies, waits for them, and re-layouts  1.94 us (2%)
    pallas_call x1, Pallas kernels, on_device(): pl.pallas_call(body, out_shape=(jax.ShapeDtypeStruct(start_vectors.shape,...  94.5 us

profile of v3, /device:TPU:1, one launch (start us, length us, event | category | flops | bytes accessed | tf_op | source)
XLA Modules:
  0.0 97.1 jit_solution(2405971173095760079)
XLA Ops:
  0.6 94.5 %shard_map.68 = (f32[64,128]{1,0:T(8,128)S(1)}, bf16[1024,1024]{1,0:T(8,128)(2,1)S(1)}) custom-call(bf16[1024,1024]{1,0:T(8,128)(2,1)} %before.1, bf16[64,512]{1,0:T(8,128)(2,1)} %panel_in.1, f32[1,1024]{1,0:T(1,128)} %bitcast.2, s32[1,512]{1,0:T(1,128)} %bitcast.3, f32[64,128]{1,0:T(8,128)} %start_in.1), custom_call_target="tpu_custom_call" | custom-call | tf_op jit(solution)/shard_map/pallas_call | solution.py:442
  95.2 0.6 copy.9
  95.8 1.3 %copy.10 = bf16[1024,1024]{1,0:T(8,128)(2,1)} copy(bf16[1024,1024]{1,0:T(8,128)(2,1)S(1)} %get-tuple-element.5) | data formatting | bytes 4194304

commit v4 on v3

--- a/solution.py
+++ b/solution.py
@@ -12,20 +12,23 @@
 N = 16
 ROWS = 64
 ZONE = 512
-WINDOW = 2
+WINDOW = 4
 
 
 def farthest_first(moves, hops):
     return sorted(moves, key=lambda move: -hops(*move))
 
 
-ROW_MOVES = farthest_first(
-    [(dx, dy, dk) for dx in (2, 1, -1, 0) for dy in (1, 0) for dk in (1, 0) if dx or dy or dk],
-    lambda dx, dy, dk: abs(dx) + dy,
-)
-NEAR = (2, -2, 1, -1)
-OTHERS = ((1, 3), (1, -3), (0, 4), (0, 3), (0, -3), (1, 0))
-PLANE_MOVES = [move for move in ROW_MOVES if move[2] == 0]
+MOVES = {
+    "row": farthest_first(
+        [(dx, dy, dk) for dx in (2, 1, -1, 0) for dy in (1, 0) for dk in (1, 0) if dx or dy or dk],
+        lambda dx, dy, dk: abs(dx) + dy,
+    ),
+    "col": farthest_first(
+        [(dy, dz) for dy in (1, 0) for dz in (4, 3, -3, 2, -2, 1, -1, 0) if dy or dz],
+        lambda dy, dz: 2 * dy + abs(dz),
+    ),
+}
 f32 = jnp.float32
 bf16 = jnp.bfloat16
 
@@ -42,9 +45,9 @@
 def body(
     before, panel_in, source_in, pixels_in, start_in, filtered, tile,
     panel, source, pixels, start, left, right, gathered, partial, arrived, outgoing,
-    whole, history, crossed, joined,
+    whole, history,
     tcc_sem, quad_send, quad_recv, ring_send, ring_recv, turn_send,
-    piece_send, piece_recv, gather_send, gather_recv, pass_send, pass_recv, sum_send, sum_recv, cross_recv,
+    piece_send, piece_recv, relay_send, relay_recv, gather_send, gather_recv, sum_send, sum_recv,
 ):
     row, col = lax.axis_index("row"), lax.axis_index("col")
     x, y_lo, core = row // 4, lax.rem(row // 2, 2), lax.rem(row, 2)
@@ -188,16 +191,33 @@
         there = piece_of(q, z)
         remote(there, there, quad_send.at[q], quad_recv.at[q], here).wait_recv()
 
+    def travelling(q, zz):
+        if q == 1:
+            return left.at[1 - half, y_hi, zz, pl.ds(0, 32), pl.ds(0, ZONE)]
+        if q == 2:
+            return left.at[half, 1 - y_hi, zz, pl.ds(0, 32)]
+        return piece_of(q, zz)
+
+    def relay(way, step, q, arriving):
+        h, yh = (half, y_hi) if not arriving else (1 - half, y_hi) if q == 1 else (half, 1 - y_hi)
+        zz, upper = mod(z - step - 1 if way == 0 else z + step + 1, 8), pl.ds(32, 32)
+        at = left.at[h, yh, zz, upper, pl.ds(0, ZONE)] if q == 1 else left.at[h, yh, zz, upper]
+        to = here if arriving else device(x + 2 * (q % 2), y + 2 * (q // 2), core, z)
+        return remote(at, at, relay_send.at[way, step, q - 1], relay_recv.at[way, step, q - 1], to)
+
     def ring(way, step, q):
-        at = piece_of(q, mod(z - step if way == 0 else z + step, 8))
+        at = travelling(q, mod(z - step if way == 0 else z + step, 8))
         return remote(
             at, at, ring_send.at[way, step, q], ring_recv.at[way, step, q],
             device(x, y, core, z + 1 if way == 0 else z + 7),
         )
 
     def ring_wait(way, step, q):
-        at = piece_of(q, mod(z - step - 1 if way == 0 else z + step + 1, 8))
+        at = travelling(q, mod(z - step - 1 if way == 0 else z + step + 1, 8))
         remote(at, at, ring_send.at[way, step, q], ring_recv.at[way, step, q], here).wait_recv()
+        if q == 0:
+            for partner in (1, 2):
+                relay(way, step, partner, False).start()
 
     in_flight = [[], []]
 
@@ -207,27 +227,34 @@
         ring(way, step, q).start()
         in_flight[way].append((step, q))
 
-    def ring_step(step):
-        for q in range(4):
-            if step == 0 and q > 0:
-                quad_wait(q)
-            for way in (0, 1):
-                if step > 0:
-                    ring_wait(way, step - 1, q)
-                if step < 3 or (q < 2) == (way == 0):
-                    ring_start(way, step, q)
+    def ring_go(step, q):
+        if step == 0 and q > 0:
+            quad_wait(q)
+        for way in (0, 1):
+            if step > 0:
+                ring_wait(way, step - 1, q)
+            if step < 3 or (q < 2) == (way == 0):
+                ring_start(way, step, q)
 
     for q in (1, 2, 3):
         quad(q).start()
-    ring_step(0)
+    for q in range(4):
+        ring_go(0, q)
     piece_first()
-    ring_step(1)
+    for q in range(4):
+        ring_go(1, q)
     piece_second()
-    ring_step(2)
+    for q in range(4):
+        ring_go(2, q)
+    for q in range(4):
+        ring_go(3, q)
     piece_third()
-    ring_step(3)
     piece_last()
     load.wait()
+    for step in range(3):
+        for way in (0, 1):
+            for partner in (1, 2):
+                relay(way, step, partner, True).wait_recv()
 
     sign = jnp.where(half == y_hi, 1.0, -1.0).astype(f32)
     nt = (((1,), (1,)), ((), ()))
@@ -245,14 +272,16 @@
         )
         tile[span] = (tile[span].astype(f32) + (straight + sign * turned)).astype(bf16)
 
+    ring_wait(0, 3, 0)
+
     @pl.loop(0, 2)
     def _(yh):
         update(yh, z // 4)
 
-    for q in range(4):
-        for way in (0, 1):
-            if (q < 2) == (way == 0):
-                ring_wait(way, 3, q)
+    for way, q in ((1, 2), (0, 1), (1, 3)):
+        ring_wait(way, 3, q)
+    for partner in (1, 2):
+        relay(0, 3, partner, True).wait_recv()
 
     @pl.loop(0, 2)
     def _(yh):
@@ -265,133 +294,37 @@
         dy, dz = move
         return 8 * mod(y_hi + dy, 2) + mod(z + dz, 8)
 
-    def back(axis, move):
-        return tuple(-d for d in move)
-
     def address(axis, index):
         return (index, col) if axis == "row" else (row, index)
 
     def rows_of(index):
         return pl.ds(pl.multiple_of(index * ROWS, ROWS), ROWS)
 
-    def piece_ref(stage, index):
-        return partial.at[stage, index // 2, lax.rem(index, 2)]
-
-    partner = (row, member("col", (1, 0)))
-
-    def gather_col(stage):
-        at = gathered.at[stage, rows_of(col)]
-        gathered[stage, rows_of(col)] = outgoing[stage]
-
-        def copy(recv, move):
-            remote(outgoing.at[stage], at, gather_send.at[0], recv, address("col", member("col", move))).start()
-
-        copy(gather_recv.at[4], (1, 4))
-        for n, dz in enumerate(NEAR):
-            copy(gather_recv.at[n], (0, dz))
-        for move in OTHERS:
-            copy(gather_recv.at[4], move)
-
-        def wait():
-            for n, dz in reversed(list(enumerate(NEAR))):
-                near = gathered.at[stage, rows_of(member("col", (0, -dz)))]
-                remote(near, near, gather_send.at[0], gather_recv.at[n], here).wait_recv()
-                remote(near, near, gather_send.at[0], gather_recv.at[4], partner).start()
-            rest = gathered.at[stage, pl.ds(0, 11 * ROWS)]
-            remote(rest, rest, gather_send.at[0], gather_recv.at[4], here).wait_recv()
-            sent = gathered.at[stage, pl.ds(0, 15 * ROWS)]
-            remote(sent, sent, gather_send.at[0], gather_recv.at[4], here).wait_send()
-
-        return wait
-
-    def gather_row(stage):
-        which = stage // 2
-
-        def copy(n, move):
-            at = gathered.at[stage, rows_of(row)]
-            return remote(
-                outgoing.at[stage], at, pass_send.at[which, n], pass_recv.at[which, n],
-                address("row", member("row", move)),
-            )
-
-        def across(n, move):
-            at = gathered.at[stage, rows_of(member("row", back("row", move)))]
-            return remote(at, at, pass_send.at[which, 7 + n], pass_recv.at[which, 7 + n], sibling)
-
-        gathered[stage, rows_of(row)] = outgoing[stage]
-        across(7, (0, 0, 0)).start()
-        for n, move in enumerate(PLANE_MOVES):
-            copy(n, move).start()
-
-        def wait():
-            for n, move in reversed(list(enumerate(PLANE_MOVES))):
-                at = gathered.at[stage, rows_of(member("row", back("row", move)))]
-                remote(at, at, pass_send.at[which, n], pass_recv.at[which, n], here).wait_recv()
-                across(n, move).start()
-            for n in range(8):
-                move = PLANE_MOVES[n] if n < 7 else (0, 0, 0)
-                at = gathered.at[stage, rows_of(row + 1 - 2 * core)]
-                remote(at, at, pass_send.at[which, n], pass_recv.at[which, 7 + n], here).wait_recv()
-            for n, move in enumerate(PLANE_MOVES):
-                copy(n, move).wait_send()
-                across(n, move).wait_send()
-            across(7, (0, 0, 0)).wait_send()
-
-        return wait
-
-    def all_sent(stage):
-        every = arrived.at[stage]
-        remote(every, every, sum_send.at[stage], sum_recv.at[stage], here).wait_send()
-
-    def sum_row(stage):
-        which = stage // 2
-        theirs = partial.at[stage, :, 1 - core]
-        remote(theirs, crossed.at[which], sum_send.at[stage], cross_recv.at[which], sibling).start()
-        remote(theirs, crossed.at[which], sum_send.at[stage], cross_recv.at[which], here).wait_recv()
-        both = whole[:, core] + crossed[which].astype(f32)
-        joined[which] = both.astype(bf16)
-        whole[:, core] = both
-        for n, move in enumerate(PLANE_MOVES):
-            to = member("row", move)
+    def gather(stage, axis):
+        me = row if axis == "row" else col
+        at = gathered.at[stage, rows_of(me)]
+        gathered[stage, rows_of(me)] = outgoing[stage]
+        for move in MOVES[axis]:
             remote(
-                joined.at[which, to // 2], arrived.at[stage, n], sum_send.at[stage], sum_recv.at[stage],
-                address("row", to),
+                outgoing.at[stage], at, gather_send.at[stage], gather_recv.at[stage], address(axis, member(axis, move))
+            ).start()
+        every = gathered.at[stage, pl.ds(0, (N - 1) * ROWS)]
+        remote(every, every, gather_send.at[stage], gather_recv.at[stage], here).wait()
+
+    def total_of(stage, axis):
+        me = row if axis == "row" else col
+        for n, move in enumerate(MOVES[axis]):
+            to = member(axis, move)
+            remote(
+                partial.at[stage, rows_of(to)], arrived.at[stage, n], sum_send.at[stage], sum_recv.at[stage],
+                address(axis, to),
             ).start()
         if stage == 0:
             panels_sent()
-        mine = whole[row // 2, core]
-        every = arrived.at[stage, pl.ds(0, 7)]
-        remote(every, every, sum_send.at[stage], sum_recv.at[stage], here).wait_recv()
-        all_sent(stage)
-        return mine + jnp.sum(arrived[stage, :7].astype(f32), axis=0)
-
-    def sum_col(stage):
-        which = 2 + stage // 2
-
-        def copy(src, slot, move):
-            remote(
-                src, arrived.at[stage, slot], sum_send.at[stage], sum_recv.at[stage], address("col", member("col", move))
-            ).start()
-
-        copy(piece_ref(stage, member("col", (1, 4))), 0, (1, 4))
-        for n, dz in enumerate(NEAR):
-            remote(
-                piece_ref(stage, member("col", (1, dz))), crossed.at[which, n], sum_send.at[stage],
-                cross_recv.at[which], partner,
-            ).start()
-        for n, move in enumerate(OTHERS):
-            copy(piece_ref(stage, member("col", move)), 1 + n, move)
-        some = crossed.at[which, pl.ds(0, 4)]
-        remote(some, some, sum_send.at[stage], cross_recv.at[which], here).wait_recv()
-        for n, dz in enumerate(NEAR):
-            to = member("col", (0, dz))
-            joined[which, n] = (whole[to // 2, lax.rem(to, 2)] + crossed[which, n].astype(f32)).astype(bf16)
-            copy(joined.at[which, n], 7 + n, (0, dz))
-        mine = whole[col // 2, lax.rem(col, 2)]
-        every = arrived.at[stage, pl.ds(0, 11)]
-        remote(every, every, sum_send.at[stage], sum_recv.at[stage], here).wait_recv()
-        all_sent(stage)
-        return mine + jnp.sum(arrived[stage, :11].astype(f32), axis=0)
+        mine = whole[rows_of(me)]
+        every = arrived.at[stage]
+        remote(every, every, sum_send.at[stage], sum_recv.at[stage], here).wait()
+        return mine + jnp.sum(arrived[stage].astype(f32), axis=0)
 
     def panels_sent():
         for q in (1, 2, 3):
@@ -404,6 +337,9 @@
         for way in (0, 1):
             for step, q in in_flight[way]:
                 ring(way, step, q).wait_send()
+            for step in range(4 - way):
+                for q in (1, 2):
+                    relay(way, step, q, False).wait_send()
         piece_sent()
 
     centre = jnp.where(row == col, CENTER, 0.0).astype(f32)
@@ -411,17 +347,16 @@
         if stage == 0:
             vectors = left[half, :, :, :, ZONE:].reshape(1024, 128)
         else:
-            wait = gather_col(stage) if stage % 2 == 0 else gather_row(stage)
-            wait()
+            gather(stage, "col" if stage % 2 == 0 else "row")
             vectors = gathered[stage]
         if stage % 2 == 0:
             image = jnp.dot(vectors.T, tile[...], preferred_element_type=f32).T
         else:
             image = jnp.dot(tile[...], vectors, preferred_element_type=f32)
         image = image - centre * vectors.astype(f32)
-        partial[stage] = image.astype(bf16).reshape(8, 2, ROWS, 128)
-        whole[...] = image.reshape(8, 2, ROWS, 128)
-        total = sum_row(stage) if stage % 2 == 0 else sum_col(stage)
+        partial[stage] = image.astype(bf16)
+        whole[...] = image
+        total = total_of(stage, "row" if stage % 2 == 0 else "col")
         if stage == 0:
             following = total / HALF_WIDTH
         else:
@@ -455,16 +390,14 @@
             pltpu.VMEM((2, 2, 8, ROWS, ZONE + 128), bf16),
             pltpu.VMEM((2, 2, 8, ROWS, ZONE), bf16),
             pltpu.VMEM((DEGREES, 1024, 128), bf16),
-            pltpu.VMEM((DEGREES, 8, 2, ROWS, 128), bf16),
+            pltpu.VMEM((DEGREES, 1024, 128), bf16),
             pltpu.VMEM((DEGREES, N - 1, ROWS, 128), bf16),
             pltpu.VMEM((DEGREES, ROWS, 128), bf16),
-            pltpu.VMEM((8, 2, ROWS, 128), f32),
+            pltpu.VMEM((1024, 128), f32),
             pltpu.VMEM((DEGREES - 1, ROWS, 128), f32),
-            pltpu.VMEM((DEGREES, 8, ROWS, 128), bf16),
-            pltpu.VMEM((DEGREES, 8, ROWS, 128), bf16),
             dma((5,)), dma((4,)), dma((4,)), dma((2, 4, 4)), dma((2, 4, 4)), dma((1,)),
-            dma((4, 4, 7)), dma((2, 2, 8)), dma((1,)), dma((5,)), dma((2, 15)), dma((2, 15)),
-            dma((DEGREES,)), dma((DEGREES,)), dma((DEGREES,)),
+            dma((4, 4, 7)), dma((2, 2, 8)), dma((2, 4, 2)), dma((2, 4, 2)),
+            dma((DEGREES,)), dma((DEGREES,)), dma((DEGREES,)), dma((DEGREES,)),
         ],
         compiler_params=pltpu.CompilerParams(
             collective_id=0, has_side_effects=True, vmem_limit_bytes=32 * 1024 * 1024

time: 97.2 us -> 93 us (0.957)
  Pallas kernels: 94.5 us -> 90.4 us
    pallas_call x1, Pallas kernels: 94.5 us -> 90.4 us  [on_device(): pl.pallas_call(body, out_shape=(jax.ShapeDtypeStruct(start_vectors.shape,...]
where the time goes in v4:
time: 93 us; the launch traced here: 92.9 us
  Pallas kernels  90.4 us (97%)
  local copies, waits for them, and re-layouts  1.94 us (2%)
    pallas_call x1, Pallas kernels, on_device(): pl.pallas_call(body, out_shape=(jax.ShapeDtypeStruct(start_vectors.shape,...  90.4 us
    unnamed x2, local copies, waits for them, and re-layouts  1.94 us

profile of v4, /device:TPU:1, one launch (start us, length us, event | category | flops | bytes accessed | tf_op | source)
XLA Modules:
  0.0 92.9 jit_solution(8429417587253493147)
XLA Ops:
  0.6 90.4 %shard_map.68 = (f32[64,128]{1,0:T(8,128)S(1)}, bf16[1024,1024]{1,0:T(8,128)(2,1)S(1)}) custom-call(bf16[1024,1024]{1,0:T(8,128)(2,1)} %before.1, bf16[64,512]{1,0:T(8,128)(2,1)} %panel_in.1, f32[1,1024]{1,0:T(1,128)} %bitcast.2, s32[1,512]{1,0:T(1,128)} %bitcast.3, f32[64,128]{1,0:T(8,128)} %start_in.1), custom_call_target="tpu_custom_call" | custom-call | tf_op jit(solution)/shard_map/pallas_call | solution.py:377
  91.0 0.6 copy.9
  91.6 1.3 %copy.10 = bf16[1024,1024]{1,0:T(8,128)(2,1)} copy(bf16[1024,1024]{1,0:T(8,128)(2,1)S(1)} %get-tuple-element.5) | data formatting | bytes 4194304

commit v5 on v4

--- a/solution.py
+++ b/solution.py
@@ -311,18 +311,46 @@
         every = gathered.at[stage, pl.ds(0, (N - 1) * ROWS)]
         remote(every, every, gather_send.at[stage], gather_recv.at[stage], here).wait()
 
-    def total_of(stage, axis):
-        me = row if axis == "row" else col
-        for n, move in enumerate(MOVES[axis]):
-            to = member(axis, move)
-            remote(
-                partial.at[stage, rows_of(to)], arrived.at[stage, n], sum_send.at[stage], sum_recv.at[stage],
-                address(axis, to),
-            ).start()
-        if stage == 0:
-            panels_sent()
+    centre = jnp.where(row == col, CENTER, 0.0).astype(f32)
+
+    def products(stage):
+        if stage % 2 == 0:
+            turned_vectors = gathered[stage].T
+            blocks = [
+                (mod(x + dx, 4), [move for move in MOVES["row"] if move[0] == dx]) for dx in (2, 1, -1, 0)
+            ]
+        else:
+            blocks = [
+                (
+                    2 * mod(y_hi + dy, 2) + (1 - z // 4 if away else z // 4),
+                    [(dy, away, t) for t in ((0, 1, 3, 2) if away else (2, 1, 3, 0)) if dy or away or t],
+                )
+                for dy in (1, 0) for away in (True, False)
+            ]
+        for place, moves in blocks:
+            span = pl.ds(pl.multiple_of(256 * place, 256), 256)
+            if stage % 2 == 0:
+                image = jnp.dot(turned_vectors, tile[:, span], preferred_element_type=f32).T
+            else:
+                image = jnp.dot(tile[span], gathered[stage], preferred_element_type=f32)
+            image = image - centre * gathered[stage, span].astype(f32)
+            partial[stage, span] = image.astype(bf16)
+            whole[span] = image
+            for move in moves:
+                if stage % 2 == 0:
+                    me, to = row, member("row", move)
+                    target = (to, col)
+                else:
+                    me, to = col, 4 * place + mod(lax.rem(z, 4) + move[2], 4)
+                    target = (row, to)
+                remote(
+                    partial.at[stage, rows_of(to)], arrived.at[stage, me], sum_send.at[stage], sum_recv.at[stage], target
+                ).start()
+
+    def total_of(stage):
+        me = row if stage % 2 == 0 else col
         mine = whole[rows_of(me)]
-        every = arrived.at[stage]
+        every = arrived.at[stage, pl.ds(0, N - 1)]
         remote(every, every, sum_send.at[stage], sum_recv.at[stage], here).wait()
         return mine + jnp.sum(arrived[stage].astype(f32), axis=0)
 
@@ -342,21 +370,16 @@
                     relay(way, step, q, False).wait_send()
         piece_sent()
 
-    centre = jnp.where(row == col, CENTER, 0.0).astype(f32)
     for stage in range(DEGREES):
+        arrived[stage, row if stage % 2 == 0 else col] = jnp.zeros((ROWS, 128), bf16)
         if stage == 0:
-            vectors = left[half, :, :, :, ZONE:].reshape(1024, 128)
+            gathered[0] = left[half, :, :, :, ZONE:].reshape(1024, 128)
         else:
             gather(stage, "col" if stage % 2 == 0 else "row")
-            vectors = gathered[stage]
-        if stage % 2 == 0:
-            image = jnp.dot(vectors.T, tile[...], preferred_element_type=f32).T
-        else:
-            image = jnp.dot(tile[...], vectors, preferred_element_type=f32)
-        image = image - centre * vectors.astype(f32)
-        partial[stage] = image.astype(bf16)
-        whole[...] = image
-        total = total_of(stage, "row" if stage % 2 == 0 else "col")
+        products(stage)
+        if stage == 0:
+            panels_sent()
+        total = total_of(stage)
         if stage == 0:
             following = total / HALF_WIDTH
         else:
@@ -391,7 +414,7 @@
             pltpu.VMEM((2, 2, 8, ROWS, ZONE), bf16),
             pltpu.VMEM((DEGREES, 1024, 128), bf16),
             pltpu.VMEM((DEGREES, 1024, 128), bf16),
-            pltpu.VMEM((DEGREES, N - 1, ROWS, 128), bf16),
+            pltpu.VMEM((DEGREES, N, ROWS, 128), bf16),
             pltpu.VMEM((DEGREES, ROWS, 128), bf16),
             pltpu.VMEM((1024, 128), f32),
             pltpu.VMEM((DEGREES - 1, ROWS, 128), f32),

time: 93 us -> 92 us (0.989)
  Pallas kernels: 90.4 us -> 89.3 us
    pallas_call x1, Pallas kernels: 90.4 us -> 89.3 us  [on_device(): pl.pallas_call(body, out_shape=(jax.ShapeDtypeStruct(start_vectors.shape,...]
where the time goes in v5:
time: 92 us; the launch traced here: 91.9 us
  Pallas kernels  89.3 us (97%)
  local copies, waits for them, and re-layouts  1.94 us (2%)
    pallas_call x1, Pallas kernels, on_device(): pl.pallas_call(body, out_shape=(jax.ShapeDtypeStruct(start_vectors.shape,...  89.3 us
    unnamed x2, local copies, waits for them, and re-layouts  1.94 us

profile of v5, /device:TPU:1, one launch (start us, length us, event | category | flops | bytes accessed | tf_op | source)
XLA Modules:
  0.0 91.9 jit_solution(2039138375150850825)
XLA Ops:
  0.6 89.3 %shard_map.68 = (f32[64,128]{1,0:T(8,128)S(1)}, bf16[1024,1024]{1,0:T(8,128)(2,1)S(1)}) custom-call(bf16[1024,1024]{1,0:T(8,128)(2,1)} %before.1, bf16[64,512]{1,0:T(8,128)(2,1)} %panel_in.1, f32[1,1024]{1,0:T(1,128)} %bitcast.2, s32[1,512]{1,0:T(1,128)} %bitcast.3, f32[64,128]{1,0:T(8,128)} %start_in.1), custom_call_target="tpu_custom_call" | custom-call | tf_op jit(solution)/shard_map/pallas_call | solution.py:400
  89.9 0.6 copy.9
  90.6 1.3 %copy.10 = bf16[1024,1024]{1,0:T(8,128)(2,1)} copy(bf16[1024,1024]{1,0:T(8,128)(2,1)S(1)} %get-tuple-element.5) | data formatting | bytes 4194304

commit v6 on v5

--- a/solution.py
+++ b/solution.py
@@ -236,7 +236,7 @@
             if step < 3 or (q < 2) == (way == 0):
                 ring_start(way, step, q)
 
-    for q in (1, 2, 3):
+    for q in (3, 1, 2):
         quad(q).start()
     for q in range(4):
         ring_go(0, q)
@@ -274,18 +274,16 @@
 
     ring_wait(0, 3, 0)
 
-    @pl.loop(0, 2)
-    def _(yh):
-        update(yh, z // 4)
-
-    for way, q in ((1, 2), (0, 1), (1, 3)):
-        ring_wait(way, 3, q)
-    for partner in (1, 2):
-        relay(0, 3, partner, True).wait_recv()
-
-    @pl.loop(0, 2)
-    def _(yh):
-        update(yh, 1 - z // 4)
+    @pl.loop(0, 4)
+    def _(i):
+        @pl.when(i == 2)
+        def _():
+            for way, q in ((1, 2), (0, 1), (1, 3)):
+                ring_wait(way, 3, q)
+            for partner in (1, 2):
+                relay(0, 3, partner, True).wait_recv()
+
+        update(lax.rem(i, 2), lax.rem(z // 4 + i // 2, 2))
 
     def member(axis, move):
         if axis == "row":
@@ -303,11 +301,11 @@
     def gather(stage, axis):
         me = row if axis == "row" else col
         at = gathered.at[stage, rows_of(me)]
-        gathered[stage, rows_of(me)] = outgoing[stage]
         for move in MOVES[axis]:
             remote(
                 outgoing.at[stage], at, gather_send.at[stage], gather_recv.at[stage], address(axis, member(axis, move))
             ).start()
+        gathered[stage, rows_of(me)] = outgoing[stage]
         every = gathered.at[stage, pl.ds(0, (N - 1) * ROWS)]
         remote(every, every, gather_send.at[stage], gather_recv.at[stage], here).wait()
 

time: 92 us -> 91 us (0.989)
  Pallas kernels: 89.3 us -> 88.1 us
    pallas_call x1, Pallas kernels: 89.3 us -> 88.1 us  [on_device(): pl.pallas_call(body, out_shape=(jax.ShapeDtypeStruct(start_vectors.shape,...]
where the time goes in v6:
time: 91 us; the launch traced here: 90.7 us
  Pallas kernels  88.1 us (97%)
  local copies, waits for them, and re-layouts  1.94 us (2%)
    pallas_call x1, Pallas kernels, on_device(): pl.pallas_call(body, out_shape=(jax.ShapeDtypeStruct(start_vectors.shape,...  88.1 us
    unnamed x2, local copies, waits for them, and re-layouts  1.94 us

profile of v6, /device:TPU:1, one launch (start us, length us, event | category | flops | bytes accessed | tf_op | source)
XLA Modules:
  0.0 90.7 jit_solution(1823541726909903829)
XLA Ops:
  0.6 88.1 %shard_map.68 = (f32[64,128]{1,0:T(8,128)S(1)}, bf16[1024,1024]{1,0:T(8,128)(2,1)S(1)}) custom-call(bf16[1024,1024]{1,0:T(8,128)(2,1)} %before.1, bf16[64,512]{1,0:T(8,128)(2,1)} %panel_in.1, f32[1,1024]{1,0:T(1,128)} %bitcast.2, s32[1,512]{1,0:T(1,128)} %bitcast.3, f32[64,128]{1,0:T(8,128)} %start_in.1), custom_call_target="tpu_custom_call" | custom-call | tf_op jit(solution)/shard_map/pallas_call | solution.py:398
  88.7 0.6 copy.9
  89.3 1.3 %copy.10 = bf16[1024,1024]{1,0:T(8,128)(2,1)} copy(bf16[1024,1024]{1,0:T(8,128)(2,1)S(1)} %get-tuple-element.5) | data formatting | bytes 4194304

commit v7 on v6

--- a/solution.py
+++ b/solution.py
@@ -157,8 +157,8 @@
                 piece_copy(i, 0, (0, d)).start()
             piece_copy(i, 0, None).start()
 
-    def piece_third():
-        for i in (0, 1, 3, 2):
+    def piece_third(which):
+        for i in which:
             for j in (1, 3, 2):
                 piece_wait(i, j)
                 piece_copy(i, j, None).start()
@@ -238,17 +238,18 @@
 
     for q in (3, 1, 2):
         quad(q).start()
-    for q in range(4):
+    for q in (0, 1, 2, 3):
         ring_go(0, q)
     piece_first()
-    for q in range(4):
+    for q in (0, 1, 2, 3):
         ring_go(1, q)
     piece_second()
-    for q in range(4):
+    for q in (0, 1, 2, 3):
         ring_go(2, q)
-    for q in range(4):
+    piece_third((0,))
+    for q in (0, 1, 2, 3):
         ring_go(3, q)
-    piece_third()
+    piece_third((1, 3, 2))
     piece_last()
     load.wait()
     for step in range(3):

time: 91 us -> 90.8 us (level)
  no operation moved by 1% of the time
where the time goes in v7:
time: 90.8 us; the launch traced here: 90.5 us
  Pallas kernels  88 us (97%)
  local copies, waits for them, and re-layouts  1.94 us (2%)
    pallas_call x1, Pallas kernels, on_device(): pl.pallas_call(body, out_shape=(jax.ShapeDtypeStruct(start_vectors.shape,...  88 us
    unnamed x2, local copies, waits for them, and re-layouts  1.94 us

profile of v7, /device:TPU:1, one launch (start us, length us, event | category | flops | bytes accessed | tf_op | source)
XLA Modules:
  0.0 90.5 jit_solution(4870242881270442038)
XLA Ops:
  0.6 88.0 %shard_map.68 = (f32[64,128]{1,0:T(8,128)S(1)}, bf16[1024,1024]{1,0:T(8,128)(2,1)S(1)}) custom-call(bf16[1024,1024]{1,0:T(8,128)(2,1)} %before.1, bf16[64,512]{1,0:T(8,128)(2,1)} %panel_in.1, f32[1,1024]{1,0:T(1,128)} %bitcast.2, s32[1,512]{1,0:T(1,128)} %bitcast.3, f32[64,128]{1,0:T(8,128)} %start_in.1), custom_call_target="tpu_custom_call" | custom-call | tf_op jit(solution)/shard_map/pallas_call | solution.py:399
  88.6 0.6 copy.9
  89.2 1.3 %copy.10 = bf16[1024,1024]{1,0:T(8,128)(2,1)} copy(bf16[1024,1024]{1,0:T(8,128)(2,1)S(1)} %get-tuple-element.5) | data formatting | bytes 4194304
